TPU v7x, 128 devices: a whole 4x4x4 slice. The times are simulated.
128 devices in a mesh: scan: 32 (over y_hi, z, x), mode: 4 (over y_lo, core).
Axes of the slice: x: 4, y: 4 (y_hi: 2, y_lo: 2; y = y_hi * 2 + y_lo), z: 4, core: 2. Of those that a mesh axis runs over, the one named last changes fastest.
Arguments:
- object_field: float32 [2, 8192, 8192], P(None, 'scan', 'mode'), may hold values from -6 to 6
- probe_modes: float32 [2, 2, 256, 256], replicated, may hold values from -3 to 3
- measured: float32 [2048, 256, 256], P(('scan', 'mode')), may hold values from 0.3 to 4
- offsets: int32 [2048, 2], P(('scan', 'mode')), may hold values from 0 to 8191, as said below
- live_count: int32 [128], P(('scan', 'mode')), may hold values from 1 to 16, as said below
Outputs:
- object_step: float32 [2, 8192, 8192], P(None, 'scan', 'mode')
- probe_step: float32 [2, 2, 256, 256], replicated
Inputs may be any that keep to these rules, and one draw needn't show every extreme that they name: `offsets`: slot q of device d = q div 16, with s = d div (4) and m = d mod (4), has its row in [s * 256, (s + 1) * 256) and its column in [m * 2048, (m + 1) * 2048); on every device one slot starts at the last row and last column of that range, and another at its first row and first column. `live_count`: the live slots of a device are its first ones; some device has all 16 slots live.
All inputs are finite; a program needn't handle non-finite values.
Results may differ from a plain program's by a relative error of at most 0.003.
The roundings to bfloat16 on the way count: a program that leaves them out, or rounds other values in their place, can miss the bound.
Values sent between devices are 32-bit elements; how exact they have to be, the bound alone decides.
No kernel may reach another device: no remote copies, remote signals or barrier semaphores. Data moves between devices by JAX's collectives and lax.ppermute only.
A program may use at most 128 MiB of HBM per device.

v0:
```python
import functools
import math

import jax
import jax.numpy as jnp
import ml_dtypes
import numpy as np
from jax import lax
from jax.experimental import pallas as pl
from jax.experimental.pallas import tpu as pltpu
from jax.sharding import PartitionSpec as P

SLOTS = 16
SIZE = 256
LANE = 128
CHUNK = 256
FLOOR = 0.5
AXES = ("scan", "mode")
f32 = jnp.float32
bf16 = jnp.bfloat16


def tables():
    n = SIZE
    place = np.arange(n)
    angles = (place[:, None] * place[None, :] % n) * (2.0 * math.pi / n)
    c = np.cos(angles) / math.sqrt(n)
    s = np.sin(angles) / math.sqrt(n)
    rows = np.concatenate([place[0 : n // 2 : 2], place[1 : n // 2 : 2]])

    def block(c, s):
        return np.block([[c, s], [-s, c]])

    def halves(c, s):
        return np.stack([block(c[rows, p::2], s[rows, p::2]) for p in (0, 1)])

    both = (halves(c, s), block(c, -s), halves(c, -s), block(c, s))
    return [t.astype(ml_dtypes.bfloat16) for t in both]


def stack(parts, axis):
    return jnp.concatenate(parts, axis)


def left_product(table, even, odd):
    dot = functools.partial(jnp.dot, preferred_element_type=f32)
    a = dot(table[0], even)
    b = dot(table[1], odd)
    return (a + b).astype(bf16), (a - b).astype(bf16)


def pattern(ext, grad, acc, probe, frame, tabs, r, c):
    left_fwd, right_fwd, left_bwd, right_bwd = tabs
    n = SIZE
    half, quarter = n // 2, n // 4
    block = c // LANE
    shift = c % LANE
    dot = functools.partial(jnp.dot, preferred_element_type=f32)

    def window(part):
        cols = []
        for j in range(3):
            view = ext.at[part, block + j]
            cols.append(stack([view[pl.ds(r + p, half, stride=2), :] for p in (0, 1)], 0))
        return pltpu.roll(stack(cols, 1), 3 * LANE - shift, 1)[:, :n]

    wr = window(0)
    wi = window(1)
    x_re = [probe[k, 0] * wr - probe[k, 1] * wi for k in (0, 1)]
    x_im = [probe[k, 0] * wi + probe[k, 1] * wr for k in (0, 1)]

    def rows_of(p):
        rows = slice(half * p, half * (p + 1))
        return stack([stack([x_re[k][rows], x_im[k][rows]], 0) for k in (0, 1)], 1).astype(bf16)

    sums = left_product(left_fwd, rows_of(0), rows_of(1))
    h = stack(
        [
            stack([t[:half, n * k : n * (k + 1)], t[half:, n * k : n * (k + 1)]], 1)
            for k in (0, 1)
            for t in sums
        ],
        0,
    )
    far = dot(h, right_fwd[...])
    sq = far * far
    intensity = (sq[:n, :n] + sq[:n, n:]) + (sq[n:, :n] + sq[n:, n:])
    amplitude = stack(
        [
            stack([frame.at[b][pl.ds(row, quarter, stride=2), :] for b in (0, 1)], 1)
            for row in (0, 1, half, half + 1)
        ],
        0,
    )
    factor = amplitude * lax.rsqrt(jnp.maximum(intensity, FLOOR)) - 1.0
    change = [
        [(far[n * k : n * (k + 1), n * p : n * (p + 1)] * factor).astype(bf16) for p in (0, 1)]
        for k in (0, 1)
    ]

    def quarters(q):
        return stack(
            [
                stack([change[k][p][at : at + quarter] for p in (0, 1) for at in (q, q + half)], 0)
                for k in (0, 1)
            ],
            1,
        )

    plus, minus = left_product(left_bwd, quarters(0), quarters(quarter))
    h = stack(
        [
            stack(
                [
                    t[at : at + quarter, n * k : n * (k + 1)],
                    t[half + at : half + at + quarter, n * k : n * (k + 1)],
                ],
                1,
            )
            for k in (0, 1)
            for t, at in ((plus, 0), (minus, 0), (plus, quarter), (minus, quarter))
        ],
        0,
    )
    delta = dot(h, right_bwd[...])
    terms = [None, None]
    for k in (0, 1):
        d_re = delta[n * k : n * k + n, :n]
        d_im = delta[n * k : n * k + n, n:]
        new = (
            probe[k, 0] * d_re + probe[k, 1] * d_im,
            probe[k, 0] * d_im - probe[k, 1] * d_re,
        )
        terms = [b if a is None else a + b for a, b in zip(terms, new)]
        acc[k, 0] += wr * d_re + wi * d_im
        acc[k, 1] += wr * d_im - wi * d_re
    blank = jnp.zeros((n, LANE), f32)
    for part, term in enumerate(terms):
        moved = pltpu.roll(stack([term, blank], 1), shift, 1)
        for j in range(3):
            view = grad.at[part, block + j]
            for p in (0, 1):
                rows = pl.ds(r + p, half, stride=2)
                view[rows, :] = view[rows, :] + moved[half * p : half * (p + 1), LANE * j : LANE * (j + 1)]


def group_kernel(first, count, homes, n_after, last, live, off, *refs):
    wide = count + 2
    refs = list(refs)
    sources = refs[: len(homes[2])]
    refs = refs[len(homes[2]) + n_after :]
    measured, probe, t0, t1, t2, t3, carry, acc_in = refs[:8]
    if last:
        upper, lower, over_upper, over_lower, acc = refs[8:13]
    else:
        upper, lower, carry_out, acc = refs[8:12]
    ext, grad, frame, picked, load_sem, frame_sem = refs[-6:]

    def pick(q, n):
        b = off[q, 1] // LANE - first
        picked[n] = q
        return n + jnp.where((b >= 0) & (b < count), 1, 0)

    n = lax.fori_loop(0, live[0], pick, jnp.int32(0))

    def loads():
        out = []
        for half in (0, 1):
            for b in range(wide):
                which, row, at = homes[half][b]
                src = sources[which].at[:, row : row + SIZE, at : at + LANE]
                dst = ext.at[:, b, SIZE * half : SIZE * (half + 1), :]
                out.append(pltpu.make_async_copy(src, dst, load_sem.at[2 * b + half]))
        return out

    def frame_copies(i):
        slot = i % 2
        return [
            pltpu.make_async_copy(
                measured.at[picked[i], :, LANE * b : LANE * (b + 1)],
                frame.at[slot, b],
                frame_sem.at[2 * slot + b],
            )
            for b in (0, 1)
        ]

    @pl.when(n > 0)
    def _():
        for copy in loads():
            copy.start()
        for copy in frame_copies(0):
            copy.start()

    grad[:, 0:2] = carry[...]
    grad[:, 2:] = jnp.zeros((2, count, 2 * SIZE, LANE), f32)
    acc[...] = acc_in[...]

    @pl.when(n > 0)
    def _():
        for copy in loads():
            copy.wait()

    def step(i, _):
        @pl.when(i + 1 < n)
        def _():
            for copy in frame_copies(i + 1):
                copy.start()

        for copy in frame_copies(i):
            copy.wait()
        q = picked[i]
        pattern(
            ext, grad, acc, probe, frame.at[i % 2], (t0, t1, t2, t3), off[q, 0], off[q, 1] - first * LANE
        )
        return 0

    lax.fori_loop(0, n, step, 0)
    upper[...] = grad[:, 0:count, :SIZE]
    lower[...] = grad[:, 0:count, SIZE:]
    if not last:
        carry_out[...] = grad[:, count:]
    if last:
        over_upper[...] = grad[:, count:, :SIZE]
        over_lower[...] = grad[:, count:, SIZE:]
        for k in (0, 1):
            for part in (0, 1):
                for b in (0, 1):
                    view = ext.at[part, 2 * k + b]
                    at = slice(LANE * b, LANE * (b + 1))
                    for p in (0, 1):
                        rows = pl.ds(p, SIZE // 2, stride=2)
                        view[rows, :] = acc[k, part, LANE * p : LANE * (p + 1), at]
                    acc[k, part, :, at] = view[0:SIZE, :]


IN_HBM = pl.BlockSpec(memory_space=pltpu.HBM)
IN_SMEM = pl.BlockSpec(memory_space=pltpu.SMEM)
IN_VMEM = pl.BlockSpec(memory_space=pltpu.VMEM)


def run_group(first, count, bounds, live, off, field, halos, corner, measured, probe, tabs, carry, acc, after):
    wide = count + 2
    arrays, homes = [], [[], []]

    def index_in(array):
        for i, other in enumerate(arrays):
            if other is array:
                return i
        arrays.append(array)
        return len(arrays) - 1

    for b in range(first, first + wide):
        if b < bounds[-1]:
            chunk = next(i for i, end in enumerate(bounds) if b < end)
            begin = bounds[chunk - 1] if chunk else 0
            homes[0].append((index_in(field), 0, b * LANE))
            homes[1].append((index_in(halos[chunk]), 0, (b - begin) * LANE))
        else:
            at = (b - bounds[-1]) * LANE
            homes[0].append((index_in(corner), 0, at))
            homes[1].append((index_in(corner), SIZE, at))
    homes.append(arrays)
    args = [live, off, *arrays, *after, measured, probe, *tabs, carry, acc]
    specs = [IN_SMEM] * 2 + [IN_HBM] * (1 + len(arrays) + len(after)) + [IN_VMEM] * 7
    part = jax.ShapeDtypeStruct((2, count, SIZE, LANE), f32)
    last = first + count == bounds[-1]
    whole = jax.ShapeDtypeStruct((2, 2, 2 * SIZE, LANE), f32)
    edge = jax.ShapeDtypeStruct((2, 2, SIZE, LANE), f32)
    out_shape = (part, part) + ((edge, edge) if last else (whole,))
    out_shape += (jax.ShapeDtypeStruct((2, 2, SIZE, SIZE), f32),)
    return pl.pallas_call(
        functools.partial(group_kernel, first, count, (homes[0], homes[1], [None] * len(arrays)),
            len(after), last),
        out_shape=out_shape,
        in_specs=specs,
        out_specs=(IN_VMEM,) * len(out_shape),
        scratch_shapes=[
            pltpu.VMEM((2, wide, 2 * SIZE, LANE), f32),
            pltpu.VMEM((2, wide, 2 * SIZE, LANE), f32),
            pltpu.VMEM((2, 2, SIZE, LANE), f32),
            pltpu.SMEM((SLOTS + 1,), jnp.int32),
            pltpu.SemaphoreType.DMA((2 * wide,)),
            pltpu.SemaphoreType.DMA((4,)),
        ],
        compiler_params=pltpu.CompilerParams(vmem_limit_bytes=44 * 2**20),
        cost_estimate=pl.CostEstimate(flops=2**33, bytes_accessed=2**12, transcendentals=0),
        name=f"group_{first}",
    )(*args)


def finish_kernel(blocks, terms, *refs):
    out, buf, sem = refs[-3:]
    copies = []
    for at, (block, many) in enumerate(zip(blocks, terms)):
        value = None
        for which, b in many:
            term = refs[which][:, b, :SIZE]
            value = term if value is None else value + term
        buf[at] = value
        copy = pltpu.make_async_copy(
            buf.at[at], out.at[:, :, block * LANE : (block + 1) * LANE], sem.at[at]
        )
        copy.start()
        copies.append(copy)
    for copy in copies:
        copy.wait()


def finish(blocks, sources, shape, onto):
    args = [array for _, array in sources]
    terms = tuple(
        tuple(
            (i, block - first)
            for i, (first, array) in enumerate(sources)
            if first <= block < first + array.shape[1]
        )
        for block in blocks
    )
    specs = [IN_VMEM] * len(args)
    aliases = {}
    if onto is not None:
        aliases = {len(args): 0}
        args.append(onto)
        specs.append(IN_HBM)
    return pl.pallas_call(
        functools.partial(finish_kernel, tuple(blocks), terms),
        out_shape=jax.ShapeDtypeStruct(shape, f32),
        in_specs=specs,
        out_specs=IN_HBM,
        scratch_shapes=[
            pltpu.VMEM((len(blocks), 2, SIZE, LANE), f32),
            pltpu.SemaphoreType.DMA((len(blocks),)),
        ],
        input_output_aliases=aliases,
        compiler_params=pltpu.CompilerParams(vmem_limit_bytes=24 * 2**20),
        name=f"finish_{blocks[0]}",
    )(*args)


def shifted(array, axis, by, name):
    count = lax.axis_size(axis)
    pairs = [(i, i + by) for i in range(count) if 0 <= i + by < count]
    with jax.named_scope(name):
        return lax.ppermute(array, axis, pairs)


def shifted_both(array, name):
    rows, cols = (lax.axis_size(a) for a in AXES)
    pairs = [
        (i * cols + j, (i + 1) * cols + j + 1) for i in range(rows - 1) for j in range(cols - 1)
    ]
    with jax.named_scope(name):
        return lax.ppermute(array, AXES, pairs)


def place_of(index):
    s, m = divmod(index, 4)
    return [m % 2, (s // 16) * 2 + m // 2, (s // 4) % 4, s % 4]


def index_of(place):
    core, y, z, x = place
    return ((y // 2) * 16 + z * 4 + x) * 4 + (y % 2) * 2 + core


def swapped(array, axis, bits):
    pairs = []
    for i in range(128):
        place = place_of(i)
        place[axis] ^= bits
        pairs.append((i, index_of(place)))
    with jax.named_scope("swap_" + "cyzx"[axis] + str(bits)):
        return lax.ppermute(array, AXES, pairs)


def halved_sum(v, axis, here, pieces, held=None):
    v = v.reshape(pieces, -1, v.shape[-1])
    pick = functools.partial(lax.dynamic_index_in_dim, axis=0, keepdims=False)
    got = [swapped(pick(v, here ^ k), axis, k) for k in range(1, pieces)]
    if pieces == 2:
        return pick(v, here) + got[0], held
    if held is not None:
        got[0], held = lax.optimization_barrier((got[0], held))
    return (pick(v, here) + got[0]) + (got[1] + got[2]), held


def exchanged_sum(v, axis, held=None):
    a, b, c = [swapped(v, axis, k) for k in (1, 2, 3)]
    if held is not None:
        a, held = lax.optimization_barrier((a, held))
    return (v + a) + (b + c), held


def gathered(v, axis, here, pieces):
    parts = [v] + [swapped(v, axis, k) for k in range(1, pieces)]

    def part_of(i):
        which = here ^ i
        if pieces == 2:
            return jnp.where(which == 0, parts[0], parts[1])
        return jnp.where(
            which < 2,
            jnp.where(which == 0, parts[0], parts[1]),
            jnp.where(which == 2, parts[2], parts[3]),
        )

    return jnp.concatenate([part_of(i) for i in range(pieces)], 0)


BOUNDS = (5, 9, 13, 15, 16)


def shards(field, probe, measured, offsets, live):
    rows, cols = field.shape[1:]
    base = jnp.stack([lax.axis_index("scan") * rows, lax.axis_index("mode") * cols])
    off = offsets - base[None, :]
    tabs = [jnp.asarray(t) for t in tables()]
    probe_rows = probe.reshape(2, 2, 128, 2, 256).transpose(0, 1, 3, 2, 4).reshape(probe.shape)
    tie = lax.optimization_barrier
    head, rest = tie((field[:, :, : LANE * BOUNDS[0]], field))
    halos = [shifted(head, "scan", -1, "halo_0")]
    for i, (a, b) in enumerate(zip(BOUNDS[:-1], BOUNDS[1:])):
        part = rest[:, :, LANE * a : LANE * b]
        if i == 1:
            part, halos[0] = tie((part, halos[0]))
        halos.append(shifted(part, "scan", -1, f"halo_{i + 1}"))
    beside = jnp.concatenate([field[:, :, :SIZE], halos[0][:, :, :SIZE]], 1)
    corner = shifted(beside, "mode", -1, "corner")
    carry = jnp.zeros((2, 2, 2 * SIZE, LANE), f32)
    acc = jnp.zeros(probe.shape, f32)
    ends = [b - 2 for b in BOUNDS[:-1]] + [BOUNDS[-1]]
    plan = [(a, b - a) for a, b in zip([0] + ends[:-1], ends)]
    uppers, lowers, comings = [], [], []
    for i, (first, count) in enumerate(plan):
        after = {2: (0,), 3: (1, corner)}.get(i, ())
        after = [comings[j] if isinstance(j, int) else j for j in after]
        upper, lower, *rest, acc = run_group(
            first, count, BOUNDS, live, off, field, halos, corner, measured, probe_rows, tabs, carry, acc, after
        )
        uppers.append(upper)
        lowers.append(lower)
        if i + 1 < len(plan):
            carry = rest[0]
            comings.append(shifted(lower, "scan", 1, f"grad_{i}"))
    over_upper, over_lower = rest
    s, m = lax.axis_index("scan"), lax.axis_index("mode")
    core, y = m % 2, (s // 16) * 2 + m // 2
    v, _ = halved_sum(acc.reshape(1024, 256), 0, core, 2)
    v, comings[2], final = tie((v, comings[2], lowers[4]))
    comings.append(shifted(final, "scan", 1, "grad_4"))
    v, _ = halved_sum(v, 1, y, 4)
    v, comings[3], over_lower = tie((v, comings[3], over_lower))
    slant = shifted_both(over_lower, "slant")
    v, _ = exchanged_sum(v, 2)
    sources = [(first, array) for (first, _), pair in zip(plan, zip(uppers, comings)) for array in pair]
    step = finish(range(2, 13), sources[:8], field.shape, None)
    v, comings[4], step, over_upper = tie((v, comings[4], step, over_upper))
    over = shifted(over_upper, "mode", 1, "over")
    v, _ = exchanged_sum(v, 3)
    slots_all = lax.axis_size("scan") * lax.axis_size("mode") * SLOTS
    v = v * (1.0 / math.sqrt(slots_all))
    v, slant = tie((v, slant))
    v = gathered(v, 1, y, 4)
    probe_step = gathered(v, 0, core, 2).reshape(probe.shape)
    sources = sources[:2] + [(13, uppers[4]), (13, comings[4]), (0, over), (0, slant)]
    step = finish([0, 1, 13, 14, 15], sources, field.shape, step)
    return (step, probe_step)


def solution(mesh):
    in_specs = (
        P(None, "scan", "mode"),
        P(),
        P(AXES, None, None),
        P(AXES, None),
        P(AXES),
    )
    out_specs = (P(None, "scan", "mode"), P())
    return jax.shard_map(shards, mesh=mesh, in_specs=in_specs, out_specs=out_specs, check_vma=False)
```

profile of v0, /device:TPU:72, one launch (start us, length us, event | category | flops | bytes accessed | tf_op | source)
XLA Modules:
  0.0 232.3 jit_solution(10959131061064164771)
XLA Ops:
  0.6 2.5 %slice.21 = f32[2,256,640]{2,1,0:T(8,128)} slice(f32[2,256,2048]{2,1,0:T(8,128)} %refs_0_.9), slice={[0:2], [0:256], [0:640]} | slice | bytes 2621440 | tf_op jit(solution)/shard_map/slice | solution.py:420
  3.2 4.2 %collective-permute-start = (f32[2,256,640]{2,1,0:T(8,128)}, f32[2,256,640]{2,1,0:T(8,128)S(1)}, u32[]{:S(2)}, u32[]{:S(2)}) collective-permute-start(f32[2,256,640]{2,1,0:T(8,128)} %slice.21), channel_id=1, source_target_pairs={{4,0},{8,4},{12,8},{16,12},{20,16},{24,20},{28,24},{32,28},{36,32}... | collective-permute-start | bytes 3932168 | tf_op jit(solution)/shard_map/halo_0/ppermute | solution.py:344
  7.4 3.0 %fusion.1 = (f32[2,256,512]{2,1,0:T(8,128)}, f32[2,256,512]{2,1,0:T(8,128)}) fusion(f32[2,256,2048]{2,1,0:T(8,128)} %refs_0_.9), kind=kLoop, calls=%fused_computation.20 | loop fusion | bytes 4194304 | tf_op jit(solution)/shard_map/slice | solution.py:423
  10.4 2.7 %collective-permute-start.6 = (f32[2,256,512]{2,1,0:T(8,128)}, f32[2,256,512]{2,1,0:T(8,128)}, u32[]{:S(2)}, u32[]{:S(2)}) collective-permute-start(f32[2,256,512]{2,1,0:T(8,128)} %get-tuple-element.76), channel_id=1, source_target_pairs={{4,0},{8,4},{12,8},{16,12},{20,16},{24,20},{28,24},{32,28},{36,32}... | collective-permute-start | bytes 3145736 | tf_op jit(solution)/shard_map/halo_1/ppermute | solution.py:344
  14.1 1.6 reshape.17
  15.7 1.3 copy.13
  17.0 20.0 %collective-permute-done.refs_1_ = f32[2,256,640]{2,1,0:T(8,128)S(1)} collective-permute-done((f32[2,256,640]{2,1,0:T(8,128)}, f32[2,256,640]{2,1,0:T(8,128)S(1)}, u32[]{:S(2)}, u32[]{:S(2)}) %collective-permute-start) | collective-permute-done | bytes 1310752 | tf_op jit(solution)/shard_map/halo_0/ppermute | solution.py:344
  38.1 1.3 copy-done.10
  39.4 1.0 copy-done.15
  42.5 14.2 %group_0.1 = (f32[2,3,256,128]{3,2,1,0:T(8,128)S(1)}, f32[2,3,256,128]{3,2,1,0:T(8,128)S(1)}, f32[2,2,512,128]{3,2,1,0:T(8,128)S(1)}, f32[2,2,256,256]{3,2,1,0:T(8,128)S(1)}) custom-call(s32[1]{0:T(128)S(6)} %copy.15.live, s32[16,2]{1,0:T(8,128)S(1)} %broadcast_subtract_fusion.off, f32[2,256,2048]{2,1,0:T(8,128)} %refs_0_.9, f32[2,256,640]{2,1,0:T(8,128)S(1)} %copy-done.10, ...), custom_call_target="tpu_custom_call" | custom-call | flops 8589934592 | bytes 4096 | tf_op jit(solution)/shard_map/group_0/pallas_call | solution.py:271
  56.7 1.9 collective-permute-start.1
  58.6 6.0 %collective-permute-start.5 = (f32[2,256,512]{2,1,0:T(8,128)}, f32[2,256,512]{2,1,0:T(8,128)}, u32[]{:S(2)}, u32[]{:S(2)}) collective-permute-start(f32[2,256,512]{2,1,0:T(8,128)} %get-tuple-element.44), channel_id=1, source_target_pairs={{4,0},{8,4},{12,8},{16,12},{20,16},{24,20},{28,24},{32,28},{36,32}... | collective-permute-start | bytes 3145736 | tf_op jit(solution)/shard_map/halo_2/ppermute | solution.py:344
  65.7 1.9 collective-permute-start.4
  67.7 6.4 %group_3.1 = (f32[2,4,256,128]{3,2,1,0:T(8,128)S(1)}, f32[2,4,256,128]{3,2,1,0:T(8,128)}, f32[2,2,512,128]{3,2,1,0:T(8,128)S(1)}, f32[2,2,256,256]{3,2,1,0:T(8,128)S(1)}) custom-call(s32[1]{0:T(128)S(6)} %copy.15.live, s32[16,2]{1,0:T(8,128)S(1)} %broadcast_subtract_fusion.off, f32[2,256,2048]{2,1,0:T(8,128)} %refs_0_.9, f32[2,256,640]{2,1,0:T(8,128)} %copy-done.9, ...), custom_call_target="tpu_custom_call" | custom-call | flops 8589934592 | bytes 4096 | tf_op jit(solution)/shard_map/group_3/pallas_call | solution.py:271
  77.0 5.5 %collective-permute-start.7 = (f32[2,4,256,128]{3,2,1,0:T(8,128)}, f32[2,4,256,128]{3,2,1,0:T(8,128)}, u32[]{:S(2)}, u32[]{:S(2)}) collective-permute-start(f32[2,4,256,128]{3,2,1,0:T(8,128)} %get-tuple-element.47), channel_id=1, source_target_pairs={{0,4},{4,8},{8,12},{12,16},{16,20},{20,24},{24,28},{28,32},{32,36}... | collective-permute-start | bytes 3145736 | tf_op jit(solution)/shard_map/grad_1/ppermute | solution.py:344
  83.4 2.4 %collective-permute-start.2 = (f32[2,256,256]{2,1,0:T(8,128)}, f32[2,256,256]{2,1,0:T(8,128)}, u32[]{:S(2)}, u32[]{:S(2)}) collective-permute-start(f32[2,256,256]{2,1,0:T(8,128)} %slice.23), channel_id=1, source_target_pairs={{4,0},{8,4},{12,8},{16,12},{20,16},{24,20},{28,24},{32,28},{36,32}... | collective-permute-start | bytes 1572872 | tf_op jit(solution)/shard_map/halo_3/ppermute | solution.py:344
  86.5 1.9 collective-permute-start.3
  89.5 1.0 copy-done.21
  92.4 10.8 %group_7.1 = (f32[2,4,256,128]{3,2,1,0:T(8,128)S(1)}, f32[2,4,256,128]{3,2,1,0:T(8,128)}, f32[2,2,512,128]{3,2,1,0:T(8,128)S(1)}, f32[2,2,256,256]{3,2,1,0:T(8,128)S(1)}) custom-call(s32[1]{0:T(128)S(6)} %copy.15.live, s32[16,2]{1,0:T(8,128)S(1)} %broadcast_subtract_fusion.off, f32[2,256,2048]{2,1,0:T(8,128)} %refs_0_.9, ...), custom_call_target="tpu_custom_call" | custom-call | flops 8589934592 | bytes 4096 | tf_op jit(solution)/shard_map/group_7/pallas_call | solution.py:271
  106.2 5.8 %collective-permute-start.9 = (f32[2,4,256,128]{3,2,1,0:T(8,128)}, f32[2,4,256,128]{3,2,1,0:T(8,128)}, u32[]{:S(2)}, u32[]{:S(2)}) collective-permute-start(f32[2,4,256,128]{3,2,1,0:T(8,128)} %get-tuple-element.56), channel_id=1, source_target_pairs={{0,4},{4,8},{8,12},{12,16},{16,20},{20,24},{24,28},{28,32},{32,36}... | collective-permute-start | bytes 3145736 | tf_op jit(solution)/shard_map/grad_2/ppermute | solution.py:344
  112.1 7.5 %group_11.1 = (f32[2,2,256,128]{3,2,1,0:T(8,128)S(1)}, f32[2,2,256,128]{3,2,1,0:T(8,128)S(1)}, f32[2,2,512,128]{3,2,1,0:T(8,128)S(1)}, f32[2,2,256,256]{3,2,1,0:T(8,128)S(1)}) custom-call(s32[1]{0:T(128)S(6)} %copy.15.live, s32[16,2]{1,0:T(8,128)S(1)} %broadcast_subtract_fusion.off, f32[2,256,2048]{2,1,0:T(8,128)} %refs_0_.9, ...), custom_call_target="tpu_custom_call" | custom-call | flops 8589934592 | bytes 4096 | tf_op jit(solution)/shard_map/group_11/pallas_call | solution.py:271
  121.2 10.7 %group_13.1 = (f32[2,3,256,128]{3,2,1,0:T(8,128)S(1)}, f32[2,3,256,128]{3,2,1,0:T(8,128)S(1)}, f32[2,2,256,128]{3,2,1,0:T(8,128)S(1)}, f32[2,2,256,128]{3,2,1,0:T(8,128)S(1)}, f32[2,2,256,256]{3,2,1,0:T(8,128)S(1)}) custom-call(s32[1]{0:T(128)S(6)} %copy.15.live, s32[16,2]{1,0:T(8,128)S(1)} %broadcast_subtract_fusion.off, f32[2,256,2048]{2,1,0:T(8,128)} %refs_0_.9, ...), custom_call_target="tpu_custom_call" | custom-call | flops 8589934592 | bytes 4096 | tf_op jit(solution)/shard_map/group_13/pallas_call | solution.py:271
  135.4 13.7 %collective-permute-start.8 = (f32[512,256]{1,0:T(8,128)}, f32[512,256]{1,0:T(8,128)}, u32[]{:S(2)}, u32[]{:S(2)}) collective-permute-start(f32[512,256]{1,0:T(8,128)} %dynamic-slice_bitcast_fusion), channel_id=1, source_target_pairs={{0,1},{1,0},{2,3},{3,2},{4,5},{5,4},{6,7},{7,6},{8,9},{9,8},{10,11... | collective-permute-start | bytes 1572872 | tf_op jit(solution)/shard_map/swap_c1/ppermute | solution.py:373
  149.1 1.9 collective-permute-start.13
  151.1 1.3 bitcast_add_fusion
  152.4 1.9 collective-permute-start.17
  155.1 3.5 %collective-permute-start.12 = (f32[128,256]{1,0:T(8,128)S(1)}, f32[128,256]{1,0:T(8,128)}, u32[]{:S(2)}, u32[]{:S(2)}) collective-permute-start(f32[128,256]{1,0:T(8,128)S(1)} %get-tuple-element.84), channel_id=1, source_target_pairs={{0,66},{1,67},{2,64},{3,65},{4,70},{5,71},{6,68},{7,69},{8,74},{9,... | collective-permute-start | bytes 393224 | tf_op jit(solution)/shard_map/swap_y3/ppermute | solution.py:373
  158.5 3.1 %collective-permute-done.10 = f32[128,256]{1,0:T(8,128)} collective-permute-done((f32[128,256]{1,0:T(8,128)}, f32[128,256]{1,0:T(8,128)}, u32[]{:S(2)}, u32[]{:S(2)}) %collective-permute-start.10) | collective-permute-done | bytes 131104 | tf_op jit(solution)/shard_map/swap_y1/ppermute | solution.py:373
  162.7 2.2 collective-permute-done.12
  164.9 1.1 fusion
  166.0 2.2 collective-permute-done.13.refs_7_
  168.2 3.9 %collective-permute-start.16 = (f32[128,256]{1,0:T(8,128)S(1)}, f32[128,256]{1,0:T(8,128)S(1)}, u32[]{:S(2)}, u32[]{:S(2)}) collective-permute-start(f32[128,256]{1,0:T(8,128)S(1)} %fusion), channel_id=1, source_target_pairs={{0,48},{1,49},{2,50},{3,51},{4,52},{5,53},{6,54},{7,55},{8,56},{9,... | collective-permute-start | bytes 393224 | tf_op jit(solution)/shard_map/swap_z3/ppermute | solution.py:373
  172.9 1.9 collective-permute-start.22
  174.9 1.2 copy-done.4
  176.1 1.0 copy-done.8
  177.1 3.4 %finish_2.1.refs_6_ = f32[2,256,2048]{2,1,0:T(8,128)} custom-call(f32[2,3,256,128]{3,2,1,0:T(8,128)S(1)} %get-tuple-element.42.refs_0_, f32[2,3,256,128]{3,2,1,0:T(8,128)S(1)} %collective-permute-done.1.refs_3_.refs_1_, f32[2,4,256,128]{3,2,1,0:T(8,128)S(1)} %copy-done.2, f32[2,4,256,128]{3,2,1,0:T(8,128)} %collective-permute-done.7.refs_3_, ...), custom_call_target="tpu_custom_call" | custom-call | tf_op jit(solution)/shard_map/finish_2/pallas_call | solution.py:325
  180.5 20.4 %collective-permute-done.16 = f32[128,256]{1,0:T(8,128)S(1)} collective-permute-done((f32[128,256]{1,0:T(8,128)S(1)}, f32[128,256]{1,0:T(8,128)S(1)}, u32[]{:S(2)}, u32[]{:S(2)}) %collective-permute-start.16) | collective-permute-done | bytes 131104 | tf_op jit(solution)/shard_map/swap_z3/ppermute | solution.py:373
  201.1 3.4 %collective-permute-start.19 = (f32[128,256]{1,0:T(8,128)S(1)}, f32[128,256]{1,0:T(8,128)S(1)}, u32[]{:S(2)}, u32[]{:S(2)}) collective-permute-start(f32[128,256]{1,0:T(8,128)S(1)} %add_add_fusion), channel_id=1, source_target_pairs={{0,4},{1,5},{2,6},{3,7},{4,0},{5,1},{6,2},{7,3},{8,12},{9,13},{10,... | collective-permute-start | bytes 393224 | tf_op jit(solution)/shard_map/swap_x1/ppermute | solution.py:373
  204.5 4.4 %collective-permute-done.20 = f32[128,256]{1,0:T(8,128)S(1)} collective-permute-done((f32[128,256]{1,0:T(8,128)S(1)}, f32[128,256]{1,0:T(8,128)S(1)}, u32[]{:S(2)}, u32[]{:S(2)}) %collective-permute-start.20) | collective-permute-done | bytes 131104 | tf_op jit(solution)/shard_map/swap_x2/ppermute | solution.py:373
  208.9 1.6 collective-permute-done.21
  211.4 4.7 %collective-permute-start.23 = (f32[128,256]{1,0:T(8,128)S(1)}, f32[128,256]{1,0:T(8,128)}, u32[]{:S(2)}, u32[]{:S(2)}) collective-permute-start(f32[128,256]{1,0:T(8,128)S(1)} %add_multiply_fusion), channel_id=1, source_target_pairs={{0,2},{1,3},{2,0},{3,1},{4,6},{5,7},{6,4},{7,5},{8,10},{9,11},{10,... | collective-permute-start | bytes 393224 | tf_op jit(solution)/shard_map/swap_y1/ppermute | solution.py:373
  216.1 1.9 collective-permute-start.18
  218.0 1.3 collective-permute-done.24
  220.6 1.1 select_select_fusion.3
  222.5 4.3 %collective-permute-done.18.refs_4_ = f32[2,2,256,128]{3,2,1,0:T(8,128)S(1)} collective-permute-done((f32[2,2,256,128]{3,2,1,0:T(8,128)}, f32[2,2,256,128]{3,2,1,0:T(8,128)S(1)}, u32[]{:S(2)}, u32[]{:S(2)}) %collective-permute-start.18) | collective-permute-done | bytes 524320 | tf_op jit(solution)/shard_map/over/ppermute | solution.py:344
  226.8 1.0 copy-done.6
  227.8 2.3 finish_0.1
  230.1 1.1 broadcast_select_fusion.1
  (119 shorter events, 26.7 us)
Async XLA Ops:
  0.6 12.6 %copy-start.39 = (s32[16,2]{0,1:T(2,128)S(1)}, s32[16,2]{0,1:T(2,128)}, u32[]{:S(2)}) copy-start(s32[16,2]{0,1:T(2,128)} %param.12) | copy-start | bytes 388
  0.6 13.4 %copy-start.36 = (f32[2,2,256,256]{3,2,1,0:T(8,128)S(1)}, f32[2,2,256,256]{3,2,1,0:T(8,128)}, u32[]{:S(2)}) copy-start(f32[2,2,256,256]{3,2,1,0:T(8,128)} %param.10) | copy-start | bytes 3145732
  3.2 33.8 %collective-permute-start = (f32[2,256,640]{2,1,0:T(8,128)}, f32[2,256,640]{2,1,0:T(8,128)S(1)}, u32[]{:S(2)}, u32[]{:S(2)}) collective-permute-start(f32[2,256,640]{2,1,0:T(8,128)} %slice.21), channel_id=1, source_target_pairs={{4,0},{8,4},{12,8},{16,12},{20,16},{24,20},{28,24},{32,28},{36,32}... | collective-permute-start | bytes 3932168 | tf_op jit(solution)/shard_map/halo_0/ppermute | solution.py:344
  10.4 57.2 %collective-permute-start.6 = (f32[2,256,512]{2,1,0:T(8,128)}, f32[2,256,512]{2,1,0:T(8,128)}, u32[]{:S(2)}, u32[]{:S(2)}) collective-permute-start(f32[2,256,512]{2,1,0:T(8,128)} %get-tuple-element.76), channel_id=1, source_target_pairs={{4,0},{8,4},{12,8},{16,12},{20,16},{24,20},{28,24},{32,28},{36,32}... | collective-permute-start | bytes 3145736 | tf_op jit(solution)/shard_map/halo_1/ppermute | solution.py:344
  13.4 24.7 %copy-start.23 = (bf16[2,256,256]{2,1,0:T(8,128)(2,1)S(1)}, bf16[2,256,256]{2,1,0:T(8,128)(2,1)}, u32[]{:S(2)}) copy-start(bf16[2,256,256]{2,1,0:T(8,128)(2,1)} %constant.81.clone.refs_4_.refs_5_.refs_6_.refs_7_) | copy-start | bytes 786436
  37.0 1.1 copy-start.9
  38.1 1.3 copy-start.10
  42.5 22.2 %slice-start = ((f32[2,256,640]{2,1,0:T(8,128)}), f32[2,256,256]{2,1,0:T(8,128)S(1)}, s32[]{:S(2)}) async-start(f32[2,256,640]{2,1,0:T(8,128)} %copy-done.9), calls=%async_computation | async-start | bytes 1048576 | tf_op jit(solution)/shard_map/slice | solution.py:427
  42.5 22.2 %slice-start.1 = ((f32[2,256,2048]{2,1,0:T(8,128)}), f32[2,256,256]{2,1,0:T(8,128)S(1)}, s32[]{:S(2)}) async-start(f32[2,256,2048]{2,1,0:T(8,128)} %refs_0_.9), calls=%async_computation.1 | async-start | bytes 1048576 | tf_op jit(solution)/shard_map/slice | solution.py:427
  42.5 25.2 %copy-start.16 = (bf16[512,512]{1,0:T(8,128)(2,1)S(1)}, bf16[512,512]{1,0:T(8,128)(2,1)}, u32[]{:S(2)}) copy-start(bf16[512,512]{1,0:T(8,128)(2,1)} %constant.82.clone.refs_5_.refs_6_.refs_7_.refs_8_) | copy-start | bytes 1572868
  42.5 25.2 %copy-start.20 = (bf16[512,512]{1,0:T(8,128)(2,1)S(1)}, bf16[512,512]{1,0:T(8,128)(2,1)}, u32[]{:S(2)}) copy-start(bf16[512,512]{1,0:T(8,128)(2,1)} %constant.84.clone.refs_7_.refs_8_.refs_9_.refs_10_) | copy-start | bytes 1572868
  42.5 25.2 %copy-start.24 = (bf16[2,256,256]{2,1,0:T(8,128)(2,1)S(1)}, bf16[2,256,256]{2,1,0:T(8,128)(2,1)}, u32[]{:S(2)}) copy-start(bf16[2,256,256]{2,1,0:T(8,128)(2,1)} %constant.81.clone.refs_4_.refs_5_.refs_6_.refs_7_) | copy-start | bytes 786436
  56.7 29.8 %collective-permute-start.1 = (f32[2,3,256,128]{3,2,1,0:T(8,128)S(1)}, f32[2,3,256,128]{3,2,1,0:T(8,128)S(1)}, u32[]{:S(2)}, u32[]{:S(2)}) collective-permute-start(f32[2,3,256,128]{3,2,1,0:T(8,128)S(1)} %get-tuple-element.43), channel_id=1, source_target_pairs={{0,4},{4,8},{8,12},{12,16},{16,20},{20,24},{24,28},{28,32},{32,36}... | collective-permute-start | bytes 2359304 | tf_op jit(solution)/shard_map/grad_0/ppermute | solution.py:344
  58.6 29.8 %collective-permute-start.5 = (f32[2,256,512]{2,1,0:T(8,128)}, f32[2,256,512]{2,1,0:T(8,128)}, u32[]{:S(2)}, u32[]{:S(2)}) collective-permute-start(f32[2,256,512]{2,1,0:T(8,128)} %get-tuple-element.44), channel_id=1, source_target_pairs={{4,0},{8,4},{12,8},{16,12},{20,16},{24,20},{28,24},{32,28},{36,32}... | collective-permute-start | bytes 3145736 | tf_op jit(solution)/shard_map/halo_2/ppermute | solution.py:344
  65.7 46.3 %collective-permute-start.4 = (f32[2,512,256]{2,1,0:T(8,128)}, f32[2,512,256]{2,1,0:T(8,128)}, u32[]{:S(2)}, u32[]{:S(2)}) collective-permute-start(f32[2,512,256]{2,1,0:T(8,128)} %pad_maximum_fusion), channel_id=1, source_target_pairs={{1,0},{2,1},{3,2},{5,4},{6,5},{7,6},{9,8},{10,9},{11,10},{13,12},{... | collective-permute-start | bytes 3145736 | tf_op jit(solution)/shard_map/corner/ppermute | solution.py:344
  67.7 14.8 %copy-start.34 = (f32[2,256,2048]{2,1,0:T(8,128)S(1)}, f32[2,256,2048]{2,1,0:T(8,128)}, u32[]{:S(2)}) copy-start(f32[2,256,2048]{2,1,0:T(8,128)} %refs_0_.9) | copy-start | bytes 12582916
  77.0 35.0 %collective-permute-start.7 = (f32[2,4,256,128]{3,2,1,0:T(8,128)}, f32[2,4,256,128]{3,2,1,0:T(8,128)}, u32[]{:S(2)}, u32[]{:S(2)}) collective-permute-start(f32[2,4,256,128]{3,2,1,0:T(8,128)} %get-tuple-element.47), channel_id=1, source_target_pairs={{0,4},{4,8},{8,12},{12,16},{16,20},{20,24},{24,28},{28,32},{32,36}... | collective-permute-start | bytes 3145736 | tf_op jit(solution)/shard_map/grad_1/ppermute | solution.py:344
  83.4 28.6 %collective-permute-start.2 = (f32[2,256,256]{2,1,0:T(8,128)}, f32[2,256,256]{2,1,0:T(8,128)}, u32[]{:S(2)}, u32[]{:S(2)}) collective-permute-start(f32[2,256,256]{2,1,0:T(8,128)} %slice.23), channel_id=1, source_target_pairs={{4,0},{8,4},{12,8},{16,12},{20,16},{24,20},{28,24},{32,28},{36,32}... | collective-permute-start | bytes 1572872 | tf_op jit(solution)/shard_map/halo_3/ppermute | solution.py:344
  86.5 34.7 %collective-permute-start.3 = (f32[2,256,128]{2,1,0:T(8,128)}, f32[2,256,128]{2,1,0:T(8,128)S(1)}, u32[]{:S(2)}, u32[]{:S(2)}) collective-permute-start(f32[2,256,128]{2,1,0:T(8,128)} %slice.24), channel_id=1, source_target_pairs={{4,0},{8,4},{12,8},{16,12},{20,16},{24,20},{28,24},{32,28},{36,32}... | collective-permute-start | bytes 786440 | tf_op jit(solution)/shard_map/halo_4/ppermute | solution.py:344
  88.5 1.0 copy-start.17
  92.4 19.6 %copy-start.18 = (bf16[512,512]{1,0:T(8,128)(2,1)S(1)}, bf16[512,512]{1,0:T(8,128)(2,1)}, u32[]{:S(2)}) copy-start(bf16[512,512]{1,0:T(8,128)(2,1)} %constant.82.clone.refs_5_.refs_6_.refs_7_.refs_8_) | copy-start | bytes 1572868
  92.4 19.6 %copy-start.22 = (bf16[512,512]{1,0:T(8,128)(2,1)S(1)}, bf16[512,512]{1,0:T(8,128)(2,1)}, u32[]{:S(2)}) copy-start(bf16[512,512]{1,0:T(8,128)(2,1)} %constant.84.clone.refs_7_.refs_8_.refs_9_.refs_10_) | copy-start | bytes 1572868
  92.4 19.6 %copy-start.26 = (bf16[2,256,256]{2,1,0:T(8,128)(2,1)S(1)}, bf16[2,256,256]{2,1,0:T(8,128)(2,1)}, u32[]{:S(2)}) copy-start(bf16[2,256,256]{2,1,0:T(8,128)(2,1)} %constant.81.clone.refs_4_.refs_5_.refs_6_.refs_7_) | copy-start | bytes 786436
  106.2 46.1 %collective-permute-start.9 = (f32[2,4,256,128]{3,2,1,0:T(8,128)}, f32[2,4,256,128]{3,2,1,0:T(8,128)}, u32[]{:S(2)}, u32[]{:S(2)}) collective-permute-start(f32[2,4,256,128]{3,2,1,0:T(8,128)} %get-tuple-element.56), channel_id=1, source_target_pairs={{0,4},{4,8},{8,12},{12,16},{16,20},{20,24},{24,28},{28,32},{32,36}... | collective-permute-start | bytes 3145736 | tf_op jit(solution)/shard_map/grad_2/ppermute | solution.py:344
  112.1 9.1 %copy-start.29 = (bf16[2,256,256]{2,1,0:T(8,128)(2,1)S(1)}, bf16[2,256,256]{2,1,0:T(8,128)(2,1)}, u32[]{:S(2)}) copy-start(bf16[2,256,256]{2,1,0:T(8,128)(2,1)} %constant.83.clone.refs_6_.refs_7_.refs_8_.refs_9_) | copy-start | bytes 786436
  133.6 1.8 copy-start.11
  133.6 41.2 %copy-start.2 = (f32[2,4,256,128]{3,2,1,0:T(8,128)S(1)}, f32[2,4,256,128]{3,2,1,0:T(8,128)}, u32[]{:S(2)}) copy-start(f32[2,4,256,128]{3,2,1,0:T(8,128)} %copy-done.1) | copy-start | bytes 3145732
  135.4 15.6 %collective-permute-start.8 = (f32[512,256]{1,0:T(8,128)}, f32[512,256]{1,0:T(8,128)}, u32[]{:S(2)}, u32[]{:S(2)}) collective-permute-start(f32[512,256]{1,0:T(8,128)} %dynamic-slice_bitcast_fusion), channel_id=1, source_target_pairs={{0,1},{1,0},{2,3},{3,2},{4,5},{5,4},{6,7},{7,6},{8,9},{9,8},{10,11... | collective-permute-start | bytes 1572872 | tf_op jit(solution)/shard_map/swap_c1/ppermute | solution.py:373
  149.1 19.1 %collective-permute-start.13 = (f32[2,2,256,128]{3,2,1,0:T(8,128)}, f32[2,2,256,128]{3,2,1,0:T(8,128)}, u32[]{:S(2)}, u32[]{:S(2)}) collective-permute-start(f32[2,2,256,128]{3,2,1,0:T(8,128)} %copy-done.14), channel_id=1, source_target_pairs={{0,4},{4,8},{8,12},{12,16},{16,20},{20,24},{24,28},{28,32},{32,36}... | collective-permute-start | bytes 1572872 | tf_op jit(solution)/shard_map/grad_3/ppermute | solution.py:344
  152.3 2.0 copy-start.35
  152.4 48.6 %collective-permute-start.17 = (f32[2,3,256,128]{3,2,1,0:T(8,128)}, f32[2,3,256,128]{3,2,1,0:T(8,128)}, u32[]{:S(2)}, u32[]{:S(2)}) collective-permute-start(f32[2,3,256,128]{3,2,1,0:T(8,128)} %copy-done.11), channel_id=1, source_target_pairs={{0,4},{4,8},{8,12},{12,16},{16,20},{20,24},{24,28},{28,32},{32,36}... | collective-permute-start | bytes 2359304 | tf_op jit(solution)/shard_map/grad_4/ppermute | solution.py:344
  155.0 6.6 %collective-permute-start.10 = (f32[128,256]{1,0:T(8,128)}, f32[128,256]{1,0:T(8,128)}, u32[]{:S(2)}, u32[]{:S(2)}) collective-permute-start(f32[128,256]{1,0:T(8,128)} %get-tuple-element.86), channel_id=1, source_target_pairs={{0,2},{1,3},{2,0},{3,1},{4,6},{5,7},{6,4},{7,5},{8,10},{9,11},{10,... | collective-permute-start | bytes 393224 | tf_op jit(solution)/shard_map/swap_y1/ppermute | solution.py:373
  155.1 7.6 %collective-permute-start.11 = (f32[128,256]{1,0:T(8,128)}, f32[128,256]{1,0:T(8,128)}, u32[]{:S(2)}, u32[]{:S(2)}) collective-permute-start(f32[128,256]{1,0:T(8,128)} %get-tuple-element.85), channel_id=1, source_target_pairs={{0,64},{1,65},{2,66},{3,67},{4,68},{5,69},{6,70},{7,71},{8,72},{9,... | collective-permute-start | bytes 393224 | tf_op jit(solution)/shard_map/swap_y2/ppermute | solution.py:373
  155.1 9.8 %collective-permute-start.12 = (f32[128,256]{1,0:T(8,128)S(1)}, f32[128,256]{1,0:T(8,128)}, u32[]{:S(2)}, u32[]{:S(2)}) collective-permute-start(f32[128,256]{1,0:T(8,128)S(1)} %get-tuple-element.84), channel_id=1, source_target_pairs={{0,66},{1,67},{2,64},{3,65},{4,70},{5,71},{6,68},{7,69},{8,74},{9,... | collective-permute-start | bytes 393224 | tf_op jit(solution)/shard_map/swap_y3/ppermute | solution.py:373
  168.2 12.3 %collective-permute-start.15 = (f32[128,256]{1,0:T(8,128)S(1)}, f32[128,256]{1,0:T(8,128)S(1)}, u32[]{:S(2)}, u32[]{:S(2)}) collective-permute-start(f32[128,256]{1,0:T(8,128)S(1)} %fusion), channel_id=1, source_target_pairs={{0,32},{1,33},{2,34},{3,35},{4,36},{5,37},{6,38},{7,39},{8,40},{9,... | collective-permute-start | bytes 393224 | tf_op jit(solution)/shard_map/swap_z2/ppermute | solution.py:373
  168.2 32.6 %collective-permute-start.16 = (f32[128,256]{1,0:T(8,128)S(1)}, f32[128,256]{1,0:T(8,128)S(1)}, u32[]{:S(2)}, u32[]{:S(2)}) collective-permute-start(f32[128,256]{1,0:T(8,128)S(1)} %fusion), channel_id=1, source_target_pairs={{0,48},{1,49},{2,50},{3,51},{4,52},{5,53},{6,54},{7,55},{8,56},{9,... | collective-permute-start | bytes 393224 | tf_op jit(solution)/shard_map/swap_z3/ppermute | solution.py:373
  172.1 28.7 %collective-permute-start.14 = (f32[128,256]{1,0:T(8,128)S(1)}, f32[128,256]{1,0:T(8,128)S(1)}, u32[]{:S(2)}, u32[]{:S(2)}) collective-permute-start(f32[128,256]{1,0:T(8,128)S(1)} %fusion), channel_id=1, source_target_pairs={{0,16},{1,17},{2,18},{3,19},{4,20},{5,21},{6,22},{7,23},{8,24},{9,... | collective-permute-start | bytes 393224 | tf_op jit(solution)/shard_map/swap_z1/ppermute | solution.py:373
  172.9 37.7 %collective-permute-start.22 = (f32[2,2,256,128]{3,2,1,0:T(8,128)}, f32[2,2,256,128]{3,2,1,0:T(8,128)S(1)}, u32[]{:S(2)}, u32[]{:S(2)}) collective-permute-start(f32[2,2,256,128]{3,2,1,0:T(8,128)} %copy-done.13), channel_id=1, source_target_pairs={{0,5},{1,6},{2,7},{4,9},{5,10},{6,11},{8,13},{9,14},{10,15},{12,17... | collective-permute-start | bytes 1572872 | tf_op jit(solution)/shard_map/slant/ppermute | solution.py:353
  174.9 1.2 copy-start.4
  200.9 8.0 %collective-permute-start.20 = (f32[128,256]{1,0:T(8,128)S(1)}, f32[128,256]{1,0:T(8,128)S(1)}, u32[]{:S(2)}, u32[]{:S(2)}) collective-permute-start(f32[128,256]{1,0:T(8,128)S(1)} %add_add_fusion), channel_id=1, source_target_pairs={{0,8},{1,9},{2,10},{3,11},{4,12},{5,13},{6,14},{7,15},{8,0},{9,1},... | collective-permute-start | bytes 393224 | tf_op jit(solution)/shard_map/swap_x2/ppermute | solution.py:373
  201.0 9.5 %collective-permute-start.21 = (f32[128,256]{1,0:T(8,128)S(1)}, f32[128,256]{1,0:T(8,128)S(1)}, u32[]{:S(2)}, u32[]{:S(2)}) collective-permute-start(f32[128,256]{1,0:T(8,128)S(1)} %add_add_fusion), channel_id=1, source_target_pairs={{0,12},{1,13},{2,14},{3,15},{4,8},{5,9},{6,10},{7,11},{8,4},{9,5},... | collective-permute-start | bytes 393224 | tf_op jit(solution)/shard_map/swap_x3/ppermute | solution.py:373
  201.1 9.4 %collective-permute-start.19 = (f32[128,256]{1,0:T(8,128)S(1)}, f32[128,256]{1,0:T(8,128)S(1)}, u32[]{:S(2)}, u32[]{:S(2)}) collective-permute-start(f32[128,256]{1,0:T(8,128)S(1)} %add_add_fusion), channel_id=1, source_target_pairs={{0,4},{1,5},{2,6},{3,7},{4,0},{5,1},{6,2},{7,3},{8,12},{9,13},{10,... | collective-permute-start | bytes 393224 | tf_op jit(solution)/shard_map/swap_x1/ppermute | solution.py:373
  211.4 7.9 %collective-permute-start.24 = (f32[128,256]{1,0:T(8,128)S(1)}, f32[128,256]{1,0:T(8,128)S(1)}, u32[]{:S(2)}, u32[]{:S(2)}) collective-permute-start(f32[128,256]{1,0:T(8,128)S(1)} %add_multiply_fusion), channel_id=1, source_target_pairs={{0,64},{1,65},{2,66},{3,67},{4,68},{5,69},{6,70},{7,71},{8,72},{9,... | collective-permute-start | bytes 393224 | tf_op jit(solution)/shard_map/swap_y2/ppermute | solution.py:373
  211.4 8.0 %collective-permute-start.25 = (f32[128,256]{1,0:T(8,128)S(1)}, f32[128,256]{1,0:T(8,128)S(1)}, u32[]{:S(2)}, u32[]{:S(2)}) collective-permute-start(f32[128,256]{1,0:T(8,128)S(1)} %add_multiply_fusion), channel_id=1, source_target_pairs={{0,66},{1,67},{2,64},{3,65},{4,70},{5,71},{6,68},{7,69},{8,74},{9,... | collective-permute-start | bytes 393224 | tf_op jit(solution)/shard_map/swap_y3/ppermute | solution.py:373
  211.4 9.2 %collective-permute-start.23 = (f32[128,256]{1,0:T(8,128)S(1)}, f32[128,256]{1,0:T(8,128)}, u32[]{:S(2)}, u32[]{:S(2)}) collective-permute-start(f32[128,256]{1,0:T(8,128)S(1)} %add_multiply_fusion), channel_id=1, source_target_pairs={{0,2},{1,3},{2,0},{3,1},{4,6},{5,7},{6,4},{7,5},{8,10},{9,11},{10,... | collective-permute-start | bytes 393224 | tf_op jit(solution)/shard_map/swap_y1/ppermute | solution.py:373
  216.1 10.7 %collective-permute-start.18 = (f32[2,2,256,128]{3,2,1,0:T(8,128)}, f32[2,2,256,128]{3,2,1,0:T(8,128)S(1)}, u32[]{:S(2)}, u32[]{:S(2)}) collective-permute-start(f32[2,2,256,128]{3,2,1,0:T(8,128)} %copy-done.12), channel_id=1, source_target_pairs={{0,1},{1,2},{2,3},{4,5},{5,6},{6,7},{8,9},{9,10},{10,11},{12,13},{... | collective-permute-start | bytes 1572872 | tf_op jit(solution)/shard_map/over/ppermute | solution.py:344
  222.5 7.6 %collective-permute-start.26 = (f32[512,256]{1,0:T(8,128)}, f32[512,256]{1,0:T(8,128)}, u32[]{:S(2)}, u32[]{:S(2)}) collective-permute-start(f32[512,256]{1,0:T(8,128)} %pad_maximum_fusion.2), channel_id=1, source_target_pairs={{0,1},{1,0},{2,3},{3,2},{4,5},{5,4},{6,7},{7,6},{8,9},{9,8},{10,11... | collective-permute-start | bytes 1572872 | tf_op jit(solution)/shard_map/swap_c1/ppermute | solution.py:373
  226.8 1.0 copy-start.6
  (21 other events, 19.2 us)
where the time goes:
time: 228 us; the launch traced here: 232 us
  starting transfers between devices  70.2 us (31%)
  waiting for transfers between devices  60.7 us (27%)
  Pallas kernels  55.2 us (24%)
  local copies, waits for them, and re-layouts  36.6 us (16%)
  other arithmetic  7.68 us (3%)
    pallas_call x5, Pallas kernels, run_group(): pl.pallas_call(functools.partial(group_kernel, first, count, (homes[0], h...  49.6 us
    ppermute x12, starting transfers between devices, shifted(): return lax.ppermute(array, axis, pairs)  38.2 us
    ppermute x14, waiting for transfers between devices, swapped(): return lax.ppermute(array, AXES, pairs)  34.2 us
    ppermute x14, starting transfers between devices, swapped(): return lax.ppermute(array, AXES, pairs)  30.1 us
    ppermute x12, waiting for transfers between devices, shifted(): return lax.ppermute(array, axis, pairs)  26.5 us
    unnamed x81, local copies, waits for them, and re-layouts  24.8 us
    pallas_call x2, Pallas kernels, finish(): pl.pallas_call(functools.partial(finish_kernel, tuple(blocks), terms), ou...  5.63 us
    slice x3, local copies, waits for them, and re-layouts, shards(): part = rest[:, :, LANE * a:LANE * b]  4.61 us
  transfers between devices with their start and end apart: 27, of which 11 were waited for; matrix products, arithmetic and copies ran while one was open for 6% of the time, Pallas kernels for 24%

commit v1 on v0

--- a/solution.py
+++ b/solution.py
@@ -441,26 +441,28 @@
         lowers.append(lower)
         if i + 1 < len(plan):
             carry = rest[0]
+        if i < len(plan) - 2:
             comings.append(shifted(lower, "scan", 1, f"grad_{i}"))
     over_upper, over_lower = rest
     s, m = lax.axis_index("scan"), lax.axis_index("mode")
     core, y = m % 2, (s // 16) * 2 + m // 2
     v, _ = halved_sum(acc.reshape(1024, 256), 0, core, 2)
-    v, comings[2], final = tie((v, comings[2], lowers[4]))
+    v, comings[2], later = tie((v, comings[2], lowers[3]))
+    comings.append(shifted(later, "scan", 1, "grad_3"))
+    v, _ = halved_sum(v, 1, y, 4)
+    v, comings[3], final = tie((v, comings[3], lowers[4]))
     comings.append(shifted(final, "scan", 1, "grad_4"))
-    v, _ = halved_sum(v, 1, y, 4)
-    v, comings[3], over_lower = tie((v, comings[3], over_lower))
-    slant = shifted_both(over_lower, "slant")
     v, _ = exchanged_sum(v, 2)
-    sources = [(first, array) for (first, _), pair in zip(plan, zip(uppers, comings)) for array in pair]
-    step = finish(range(2, 13), sources[:8], field.shape, None)
-    v, comings[4], step, over_upper = tie((v, comings[4], step, over_upper))
-    over = shifted(over_upper, "mode", 1, "over")
     v, _ = exchanged_sum(v, 3)
     slots_all = lax.axis_size("scan") * lax.axis_size("mode") * SLOTS
     v = v * (1.0 / math.sqrt(slots_all))
-    v, slant = tie((v, slant))
+    v, comings[4], over_lower, over_upper = tie((v, comings[4], over_lower, over_upper))
+    slant = shifted_both(over_lower, "slant")
+    sources = [(first, array) for (first, _), pair in zip(plan, zip(uppers, comings)) for array in pair]
+    step = finish(range(2, 13), sources[:8], field.shape, None)
     v = gathered(v, 1, y, 4)
+    v, step, slant = tie((v, step, slant))
+    over = shifted(over_upper, "mode", 1, "over")
     probe_step = gathered(v, 0, core, 2).reshape(probe.shape)
     sources = sources[:2] + [(13, uppers[4]), (13, comings[4]), (0, over), (0, slant)]
     step = finish([0, 1, 13, 14, 15], sources, field.shape, step)

time: 228 us -> 235 us (1.031)
  the two profiles are of different devices: /device:TPU:72 before, /device:TPU:1 now
where the time goes in v1:
time: 235 us; the launch traced here: 234 us
  starting transfers between devices  88.4 us (38%)
  waiting for transfers between devices  64.7 us (28%)
  local copies, waits for them, and re-layouts  35.8 us (15%)
  Pallas kernels  35.8 us (15%)
  other arithmetic  7.7 us (3%)
    ppermute x14, starting transfers between devices, swapped(): return lax.ppermute(array, AXES, pairs)  46 us
    ppermute x12, starting transfers between devices, shifted(): return lax.ppermute(array, axis, pairs)  38 us
    ppermute x12, waiting for transfers between devices, shifted(): return lax.ppermute(array, axis, pairs)  34.6 us
    pallas_call x5, Pallas kernels, run_group(): pl.pallas_call(functools.partial(group_kernel, first, count, (homes[0], h...  30.3 us
    ppermute x14, waiting for transfers between devices, swapped(): return lax.ppermute(array, AXES, pairs)  30.1 us
    unnamed x73, local copies, waits for them, and re-layouts  22.9 us
    pallas_call x2, Pallas kernels, finish(): pl.pallas_call(functools.partial(finish_kernel, tuple(blocks), terms), ou...  5.54 us
  transfers between devices with their start and end apart: 27, of which 11 were waited for; matrix products, arithmetic and copies ran while one was open for 7% of the time, Pallas kernels for 15%

profile of v1, /device:TPU:1, one launch (start us, length us, event | category | flops | bytes accessed | tf_op | source)
XLA Modules:
  0.0 234.2 jit_solution(6326917667501766775)
XLA Ops:
  0.6 2.5 %slice.21 = f32[2,256,640]{2,1,0:T(8,128)} slice(f32[2,256,2048]{2,1,0:T(8,128)} %refs_0_.9), slice={[0:2], [0:256], [0:640]} | slice | bytes 2621440 | tf_op jit(solution)/shard_map/slice | solution.py:420
  3.2 1.3 collective-permute-start
  4.5 3.0 %fusion.1 = (f32[2,256,512]{2,1,0:T(8,128)}, f32[2,256,512]{2,1,0:T(8,128)}) fusion(f32[2,256,2048]{2,1,0:T(8,128)} %refs_0_.9), kind=kLoop, calls=%fused_computation.20 | loop fusion | bytes 4194304 | tf_op jit(solution)/shard_map/slice | solution.py:423
  7.5 1.3 collective-permute-start.6
  9.7 1.6 reshape.17
  11.3 1.3 copy.13
  12.6 22.7 %collective-permute-done.refs_1_ = f32[2,256,640]{2,1,0:T(8,128)S(1)} collective-permute-done((f32[2,256,640]{2,1,0:T(8,128)}, f32[2,256,640]{2,1,0:T(8,128)S(1)}, u32[]{:S(2)}, u32[]{:S(2)}) %collective-permute-start) | collective-permute-done | bytes 1310752 | tf_op jit(solution)/shard_map/halo_0/ppermute | solution.py:344
  36.5 1.3 copy-done.10
  40.9 4.3 %group_0.1 = (f32[2,3,256,128]{3,2,1,0:T(8,128)S(1)}, f32[2,3,256,128]{3,2,1,0:T(8,128)S(1)}, f32[2,2,512,128]{3,2,1,0:T(8,128)S(1)}, f32[2,2,256,256]{3,2,1,0:T(8,128)S(1)}) custom-call(s32[1]{0:T(128)S(6)} %copy.15.live, s32[16,2]{1,0:T(8,128)S(1)} %broadcast_subtract_fusion.off, f32[2,256,2048]{2,1,0:T(8,128)} %refs_0_.9, f32[2,256,640]{2,1,0:T(8,128)S(1)} %copy-done.10, ...), custom_call_target="tpu_custom_call" | custom-call | flops 8589934592 | bytes 4096 | tf_op jit(solution)/shard_map/group_0/pallas_call | solution.py:271
  45.2 3.5 %collective-permute-start.1 = (f32[2,3,256,128]{3,2,1,0:T(8,128)S(1)}, f32[2,3,256,128]{3,2,1,0:T(8,128)S(1)}, u32[]{:S(2)}, u32[]{:S(2)}) collective-permute-start(f32[2,3,256,128]{3,2,1,0:T(8,128)S(1)} %get-tuple-element.44), channel_id=1, source_target_pairs={{0,4},{4,8},{8,12},{12,16},{16,20},{20,24},{24,28},{28,32},{32,36}... | collective-permute-start | bytes 2359304 | tf_op jit(solution)/shard_map/grad_0/ppermute | solution.py:344
  48.7 1.3 collective-permute-start.5
  51.1 4.9 %collective-permute-start.4 = (f32[2,512,256]{2,1,0:T(8,128)}, f32[2,512,256]{2,1,0:T(8,128)}, u32[]{:S(2)}, u32[]{:S(2)}) collective-permute-start(f32[2,512,256]{2,1,0:T(8,128)} %pad_maximum_fusion), channel_id=1, source_target_pairs={{1,0},{2,1},{3,2},{5,4},{6,5},{7,6},{9,8},{10,9},{11,10},{13,12},{... | collective-permute-start | bytes 3145736 | tf_op jit(solution)/shard_map/corner/ppermute | solution.py:344
  56.0 1.9 collective-permute-done.6.refs_2_.refs_1_
  57.9 8.2 %group_3.1 = (f32[2,4,256,128]{3,2,1,0:T(8,128)S(1)}, f32[2,4,256,128]{3,2,1,0:T(8,128)}, f32[2,2,512,128]{3,2,1,0:T(8,128)S(1)}, f32[2,2,256,256]{3,2,1,0:T(8,128)S(1)}) custom-call(s32[1]{0:T(128)S(6)} %copy.15.live, s32[16,2]{1,0:T(8,128)S(1)} %broadcast_subtract_fusion.off, f32[2,256,2048]{2,1,0:T(8,128)} %refs_0_.9, f32[2,256,640]{2,1,0:T(8,128)} %copy-done.9, ...), custom_call_target="tpu_custom_call" | custom-call | flops 8589934592 | bytes 4096 | tf_op jit(solution)/shard_map/group_3/pallas_call | solution.py:271
  69.1 2.3 collective-permute-start.7
  72.2 1.3 collective-permute-start.2
  74.2 1.3 collective-permute-start.3
  75.5 4.9 %collective-permute-done.5.refs_2_.refs_1_ = f32[2,256,512]{2,1,0:T(8,128)} collective-permute-done((f32[2,256,512]{2,1,0:T(8,128)}, f32[2,256,512]{2,1,0:T(8,128)}, u32[]{:S(2)}, u32[]{:S(2)}) %collective-permute-start.5) | collective-permute-done | bytes 1048608 | tf_op jit(solution)/shard_map/halo_2/ppermute | solution.py:344
  80.4 1.0 copy-done.16
  84.4 6.8 %group_7.1 = (f32[2,4,256,128]{3,2,1,0:T(8,128)S(1)}, f32[2,4,256,128]{3,2,1,0:T(8,128)}, f32[2,2,512,128]{3,2,1,0:T(8,128)S(1)}, f32[2,2,256,256]{3,2,1,0:T(8,128)S(1)}) custom-call(s32[1]{0:T(128)S(6)} %copy.15.live, s32[16,2]{1,0:T(8,128)S(1)} %broadcast_subtract_fusion.off, f32[2,256,2048]{2,1,0:T(8,128)} %refs_0_.9, ...), custom_call_target="tpu_custom_call" | custom-call | flops 8589934592 | bytes 4096 | tf_op jit(solution)/shard_map/group_7/pallas_call | solution.py:271
  94.1 2.7 %collective-permute-start.9 = (f32[2,4,256,128]{3,2,1,0:T(8,128)}, f32[2,4,256,128]{3,2,1,0:T(8,128)}, u32[]{:S(2)}, u32[]{:S(2)}) collective-permute-start(f32[2,4,256,128]{3,2,1,0:T(8,128)} %get-tuple-element.57), channel_id=1, source_target_pairs={{0,4},{4,8},{8,12},{12,16},{16,20},{20,24},{24,28},{28,32},{32,36}... | collective-permute-start | bytes 3145736 | tf_op jit(solution)/shard_map/grad_2/ppermute | solution.py:344
  96.8 5.4 %group_11.1 = (f32[2,2,256,128]{3,2,1,0:T(8,128)S(1)}, f32[2,2,256,128]{3,2,1,0:T(8,128)S(1)}, f32[2,2,512,128]{3,2,1,0:T(8,128)S(1)}, f32[2,2,256,256]{3,2,1,0:T(8,128)S(1)}) custom-call(s32[1]{0:T(128)S(6)} %copy.15.live, s32[16,2]{1,0:T(8,128)S(1)} %broadcast_subtract_fusion.off, f32[2,256,2048]{2,1,0:T(8,128)} %refs_0_.9, ...), custom_call_target="tpu_custom_call" | custom-call | flops 8589934592 | bytes 4096 | tf_op jit(solution)/shard_map/group_11/pallas_call | solution.py:271
  103.9 5.5 %group_13.1 = (f32[2,3,256,128]{3,2,1,0:T(8,128)S(1)}, f32[2,3,256,128]{3,2,1,0:T(8,128)S(1)}, f32[2,2,256,128]{3,2,1,0:T(8,128)}, f32[2,2,256,128]{3,2,1,0:T(8,128)S(1)}, f32[2,2,256,256]{3,2,1,0:T(8,128)S(1)}) custom-call(s32[1]{0:T(128)S(6)} %copy.15.live, s32[16,2]{1,0:T(8,128)S(1)} %broadcast_subtract_fusion.off, f32[2,256,2048]{2,1,0:T(8,128)} %refs_0_.9, ...), custom_call_target="tpu_custom_call" | custom-call | flops 8589934592 | bytes 4096 | tf_op jit(solution)/shard_map/group_13/pallas_call | solution.py:271
  112.1 2.2 collective-permute-done.8
  114.3 2.1 bitcast_add_fusion
  116.4 11.7 %collective-permute-start.13 = (f32[2,2,256,128]{3,2,1,0:T(8,128)}, f32[2,2,256,128]{3,2,1,0:T(8,128)}, u32[]{:S(2)}, u32[]{:S(2)}) collective-permute-start(f32[2,2,256,128]{3,2,1,0:T(8,128)} %copy-done.13), channel_id=1, source_target_pairs={{0,4},{4,8},{8,12},{12,16},{16,20},{20,24},{24,28},{28,32},{32,36}... | collective-permute-start | bytes 1572872 | tf_op jit(solution)/shard_map/grad_3/ppermute | solution.py:344
  128.2 1.8 dynamic-slice_bitcast_fusion.1
  129.9 7.4 %collective-permute-start.10 = (f32[128,256]{1,0:T(8,128)}, f32[128,256]{1,0:T(8,128)}, u32[]{:S(2)}, u32[]{:S(2)}) collective-permute-start(f32[128,256]{1,0:T(8,128)} %get-tuple-element.88), channel_id=1, source_target_pairs={{0,2},{1,3},{2,0},{3,1},{4,6},{5,7},{6,4},{7,5},{8,10},{9,11},{10,... | collective-permute-start | bytes 393224 | tf_op jit(solution)/shard_map/swap_y1/ppermute | solution.py:373
  137.3 23.7 %collective-permute-start.11 = (f32[128,256]{1,0:T(8,128)}, f32[128,256]{1,0:T(8,128)}, u32[]{:S(2)}, u32[]{:S(2)}) collective-permute-start(f32[128,256]{1,0:T(8,128)} %get-tuple-element.87), channel_id=1, source_target_pairs={{0,64},{1,65},{2,66},{3,67},{4,68},{5,69},{6,70},{7,71},{8,72},{9,... | collective-permute-start | bytes 393224 | tf_op jit(solution)/shard_map/swap_y2/ppermute | solution.py:373
  161.0 6.7 %collective-permute-done.11 = f32[128,256]{1,0:T(8,128)} collective-permute-done((f32[128,256]{1,0:T(8,128)}, f32[128,256]{1,0:T(8,128)}, u32[]{:S(2)}, u32[]{:S(2)}) %collective-permute-start.11) | collective-permute-done | bytes 131104 | tf_op jit(solution)/shard_map/swap_y2/ppermute | solution.py:373
  167.6 2.3 collective-permute-done.12
  169.9 1.1 fusion
  171.1 1.3 collective-permute-start.20
  172.6 2.5 %collective-permute-start.14 = (f32[128,256]{1,0:T(8,128)S(1)}, f32[128,256]{1,0:T(8,128)S(1)}, u32[]{:S(2)}, u32[]{:S(2)}) collective-permute-start(f32[128,256]{1,0:T(8,128)S(1)} %fusion), channel_id=1, source_target_pairs={{0,16},{1,17},{2,18},{3,19},{4,20},{5,21},{6,22},{7,23},{8,24},{9,... | collective-permute-start | bytes 393224 | tf_op jit(solution)/shard_map/swap_z1/ppermute | solution.py:373
  175.2 11.3 %collective-permute-done.15 = f32[128,256]{1,0:T(8,128)S(1)} collective-permute-done((f32[128,256]{1,0:T(8,128)S(1)}, f32[128,256]{1,0:T(8,128)S(1)}, u32[]{:S(2)}, u32[]{:S(2)}) %collective-permute-start.15) | collective-permute-done | bytes 131104 | tf_op jit(solution)/shard_map/swap_z2/ppermute | solution.py:373
  188.2 1.9 collective-permute-start.17
  190.1 3.5 %collective-permute-done.18 = f32[128,256]{1,0:T(8,128)S(1)} collective-permute-done((f32[128,256]{1,0:T(8,128)S(1)}, f32[128,256]{1,0:T(8,128)S(1)}, u32[]{:S(2)}, u32[]{:S(2)}) %collective-permute-start.18) | collective-permute-done | bytes 131104 | tf_op jit(solution)/shard_map/swap_x2/ppermute | solution.py:373
  193.6 3.2 %collective-permute-done.19 = f32[128,256]{1,0:T(8,128)S(1)} collective-permute-done((f32[128,256]{1,0:T(8,128)S(1)}, f32[128,256]{1,0:T(8,128)S(1)}, u32[]{:S(2)}, u32[]{:S(2)}) %collective-permute-start.19) | collective-permute-done | bytes 131104 | tf_op jit(solution)/shard_map/swap_x3/ppermute | solution.py:373
  197.7 4.3 %collective-permute-start.25 = (f32[2,2,256,128]{3,2,1,0:T(8,128)}, f32[2,2,256,128]{3,2,1,0:T(8,128)}, u32[]{:S(2)}, u32[]{:S(2)}) collective-permute-start(f32[2,2,256,128]{3,2,1,0:T(8,128)} %copy-done.12), channel_id=1, source_target_pairs={{0,5},{1,6},{2,7},{4,9},{5,10},{6,11},{8,13},{9,14},{10,15},{12,17... | collective-permute-start | bytes 1572872 | tf_op jit(solution)/shard_map/slant/ppermute | solution.py:353
  202.1 9.4 %collective-permute-start.23 = (f32[128,256]{1,0:T(8,128)S(1)}, f32[128,256]{1,0:T(8,128)}, u32[]{:S(2)}, u32[]{:S(2)}) collective-permute-start(f32[128,256]{1,0:T(8,128)S(1)} %add_multiply_fusion), channel_id=1, source_target_pairs={{0,64},{1,65},{2,66},{3,67},{4,68},{5,69},{6,70},{7,71},{8,72},{9,... | collective-permute-start | bytes 393224 | tf_op jit(solution)/shard_map/swap_y2/ppermute | solution.py:373
  211.5 1.2 copy-done.4
  213.8 3.4 %finish_2.1.refs_6_ = f32[2,256,2048]{2,1,0:T(8,128)} custom-call(f32[2,3,256,128]{3,2,1,0:T(8,128)S(1)} %get-tuple-element.43.refs_0_, f32[2,3,256,128]{3,2,1,0:T(8,128)S(1)} %collective-permute-done.1.refs_3_.refs_1_, f32[2,4,256,128]{3,2,1,0:T(8,128)S(1)} %copy-done.2, f32[2,4,256,128]{3,2,1,0:T(8,128)} %collective-permute-done.7.refs_3_, ...), custom_call_target="tpu_custom_call" | custom-call | tf_op jit(solution)/shard_map/finish_2/pallas_call | solution.py:325
  217.1 5.2 %collective-permute-start.21 = (f32[2,2,256,128]{3,2,1,0:T(8,128)}, f32[2,2,256,128]{3,2,1,0:T(8,128)S(1)}, u32[]{:S(2)}, u32[]{:S(2)}) collective-permute-start(f32[2,2,256,128]{3,2,1,0:T(8,128)} %get-tuple-element.67), channel_id=1, source_target_pairs={{0,1},{1,2},{2,3},{4,5},{5,6},{6,7},{8,9},{9,10},{10,11},{12,13},{... | collective-permute-start | bytes 1572872 | tf_op jit(solution)/shard_map/over/ppermute | solution.py:344
  222.3 1.1 select_select_fusion.3
  223.6 5.1 %collective-permute-done.21.refs_4_ = f32[2,2,256,128]{3,2,1,0:T(8,128)S(1)} collective-permute-done((f32[2,2,256,128]{3,2,1,0:T(8,128)}, f32[2,2,256,128]{3,2,1,0:T(8,128)S(1)}, u32[]{:S(2)}, u32[]{:S(2)}) %collective-permute-start.21) | collective-permute-done | bytes 524320 | tf_op jit(solution)/shard_map/over/ppermute | solution.py:344
  228.7 1.1 copy-done.6
  229.8 2.2 finish_0.1
  232.0 1.1 broadcast_select_fusion.1
  (111 shorter events, 25.1 us)
Async XLA Ops:
  0.6 8.2 %copy-start.35 = (s32[16,2]{0,1:T(2,128)S(1)}, s32[16,2]{0,1:T(2,128)}, u32[]{:S(2)}) copy-start(s32[16,2]{0,1:T(2,128)} %param.12) | copy-start | bytes 388
  0.6 9.1 %copy-start.34 = (f32[2,2,256,256]{3,2,1,0:T(8,128)S(1)}, f32[2,2,256,256]{3,2,1,0:T(8,128)}, u32[]{:S(2)}) copy-start(f32[2,2,256,256]{3,2,1,0:T(8,128)} %param.10) | copy-start | bytes 3145732
  3.2 32.1 %collective-permute-start = (f32[2,256,640]{2,1,0:T(8,128)}, f32[2,256,640]{2,1,0:T(8,128)S(1)}, u32[]{:S(2)}, u32[]{:S(2)}) collective-permute-start(f32[2,256,640]{2,1,0:T(8,128)} %slice.21), channel_id=1, source_target_pairs={{4,0},{8,4},{12,8},{16,12},{20,16},{24,20},{28,24},{32,28},{36,32}... | collective-permute-start | bytes 3932168 | tf_op jit(solution)/shard_map/halo_0/ppermute | solution.py:344
  7.5 50.4 %collective-permute-start.6 = (f32[2,256,512]{2,1,0:T(8,128)}, f32[2,256,512]{2,1,0:T(8,128)}, u32[]{:S(2)}, u32[]{:S(2)}) collective-permute-start(f32[2,256,512]{2,1,0:T(8,128)} %get-tuple-element.78), channel_id=1, source_target_pairs={{4,0},{8,4},{12,8},{16,12},{20,16},{24,20},{28,24},{32,28},{36,32}... | collective-permute-start | bytes 3145736 | tf_op jit(solution)/shard_map/halo_1/ppermute | solution.py:344
  9.0 27.5 %copy-start.22 = (bf16[2,256,256]{2,1,0:T(8,128)(2,1)S(1)}, bf16[2,256,256]{2,1,0:T(8,128)(2,1)}, u32[]{:S(2)}) copy-start(bf16[2,256,256]{2,1,0:T(8,128)(2,1)} %constant.81.clone.refs_4_.refs_5_.refs_6_.refs_7_) | copy-start | bytes 786436
  35.3 1.1 copy-start.9
  36.5 1.3 copy-start.10
  37.8 1.0 copy-start.14
  40.8 9.2 %slice-start = ((f32[2,256,640]{2,1,0:T(8,128)}), f32[2,256,256]{2,1,0:T(8,128)S(1)}, s32[]{:S(2)}) async-start(f32[2,256,640]{2,1,0:T(8,128)} %copy-done.9), calls=%async_computation | async-start | bytes 1048576 | tf_op jit(solution)/shard_map/slice | solution.py:427
  40.8 9.2 %slice-start.1 = ((f32[2,256,2048]{2,1,0:T(8,128)}), f32[2,256,256]{2,1,0:T(8,128)S(1)}, s32[]{:S(2)}) async-start(f32[2,256,2048]{2,1,0:T(8,128)} %refs_0_.9), calls=%async_computation.1 | async-start | bytes 1048576 | tf_op jit(solution)/shard_map/slice | solution.py:427
  40.8 17.1 %copy-start.15 = (bf16[512,512]{1,0:T(8,128)(2,1)S(1)}, bf16[512,512]{1,0:T(8,128)(2,1)}, u32[]{:S(2)}) copy-start(bf16[512,512]{1,0:T(8,128)(2,1)} %constant.82.clone.refs_5_.refs_6_.refs_7_.refs_8_) | copy-start | bytes 1572868
  40.8 17.1 %copy-start.19 = (bf16[512,512]{1,0:T(8,128)(2,1)S(1)}, bf16[512,512]{1,0:T(8,128)(2,1)}, u32[]{:S(2)}) copy-start(bf16[512,512]{1,0:T(8,128)(2,1)} %constant.84.clone.refs_7_.refs_8_.refs_9_.refs_10_) | copy-start | bytes 1572868
  40.8 17.1 %copy-start.23 = (bf16[2,256,256]{2,1,0:T(8,128)(2,1)S(1)}, bf16[2,256,256]{2,1,0:T(8,128)(2,1)}, u32[]{:S(2)}) copy-start(bf16[2,256,256]{2,1,0:T(8,128)(2,1)} %constant.81.clone.refs_4_.refs_5_.refs_6_.refs_7_) | copy-start | bytes 786436
  45.2 29.0 %collective-permute-start.1 = (f32[2,3,256,128]{3,2,1,0:T(8,128)S(1)}, f32[2,3,256,128]{3,2,1,0:T(8,128)S(1)}, u32[]{:S(2)}, u32[]{:S(2)}) collective-permute-start(f32[2,3,256,128]{3,2,1,0:T(8,128)S(1)} %get-tuple-element.44), channel_id=1, source_target_pairs={{0,4},{4,8},{8,12},{12,16},{16,20},{20,24},{24,28},{28,32},{32,36}... | collective-permute-start | bytes 2359304 | tf_op jit(solution)/shard_map/grad_0/ppermute | solution.py:344
  48.7 31.6 %collective-permute-start.5 = (f32[2,256,512]{2,1,0:T(8,128)}, f32[2,256,512]{2,1,0:T(8,128)}, u32[]{:S(2)}, u32[]{:S(2)}) collective-permute-start(f32[2,256,512]{2,1,0:T(8,128)} %get-tuple-element.45), channel_id=1, source_target_pairs={{4,0},{8,4},{12,8},{16,12},{20,16},{24,20},{28,24},{32,28},{36,32}... | collective-permute-start | bytes 3145736 | tf_op jit(solution)/shard_map/halo_2/ppermute | solution.py:344
  51.1 45.7 %collective-permute-start.4 = (f32[2,512,256]{2,1,0:T(8,128)}, f32[2,512,256]{2,1,0:T(8,128)}, u32[]{:S(2)}, u32[]{:S(2)}) collective-permute-start(f32[2,512,256]{2,1,0:T(8,128)} %pad_maximum_fusion), channel_id=1, source_target_pairs={{1,0},{2,1},{3,2},{5,4},{6,5},{7,6},{9,8},{10,9},{11,10},{13,12},{... | collective-permute-start | bytes 3145736 | tf_op jit(solution)/shard_map/corner/ppermute | solution.py:344
  57.9 13.4 %copy-start.33 = (f32[2,256,2048]{2,1,0:T(8,128)S(1)}, f32[2,256,2048]{2,1,0:T(8,128)}, u32[]{:S(2)}) copy-start(f32[2,256,2048]{2,1,0:T(8,128)} %refs_0_.9) | copy-start | bytes 12582916
  69.1 27.7 %collective-permute-start.7 = (f32[2,4,256,128]{3,2,1,0:T(8,128)}, f32[2,4,256,128]{3,2,1,0:T(8,128)}, u32[]{:S(2)}, u32[]{:S(2)}) collective-permute-start(f32[2,4,256,128]{3,2,1,0:T(8,128)} %get-tuple-element.48), channel_id=1, source_target_pairs={{0,4},{4,8},{8,12},{12,16},{16,20},{20,24},{24,28},{28,32},{32,36}... | collective-permute-start | bytes 3145736 | tf_op jit(solution)/shard_map/grad_1/ppermute | solution.py:344
  72.2 24.6 %collective-permute-start.2 = (f32[2,256,256]{2,1,0:T(8,128)}, f32[2,256,256]{2,1,0:T(8,128)}, u32[]{:S(2)}, u32[]{:S(2)}) collective-permute-start(f32[2,256,256]{2,1,0:T(8,128)} %slice.23), channel_id=1, source_target_pairs={{4,0},{8,4},{12,8},{16,12},{20,16},{24,20},{28,24},{32,28},{36,32}... | collective-permute-start | bytes 1572872 | tf_op jit(solution)/shard_map/halo_3/ppermute | solution.py:344
  74.2 29.7 %collective-permute-start.3 = (f32[2,256,128]{2,1,0:T(8,128)}, f32[2,256,128]{2,1,0:T(8,128)S(1)}, u32[]{:S(2)}, u32[]{:S(2)}) collective-permute-start(f32[2,256,128]{2,1,0:T(8,128)} %slice.24), channel_id=1, source_target_pairs={{4,0},{8,4},{12,8},{16,12},{20,16},{24,20},{28,24},{32,28},{36,32}... | collective-permute-start | bytes 786440 | tf_op jit(solution)/shard_map/halo_4/ppermute | solution.py:344
  80.4 1.0 copy-start.16
  84.4 12.4 %copy-start.17 = (bf16[512,512]{1,0:T(8,128)(2,1)S(1)}, bf16[512,512]{1,0:T(8,128)(2,1)}, u32[]{:S(2)}) copy-start(bf16[512,512]{1,0:T(8,128)(2,1)} %constant.82.clone.refs_5_.refs_6_.refs_7_.refs_8_) | copy-start | bytes 1572868
  84.4 12.4 %copy-start.21 = (bf16[512,512]{1,0:T(8,128)(2,1)S(1)}, bf16[512,512]{1,0:T(8,128)(2,1)}, u32[]{:S(2)}) copy-start(bf16[512,512]{1,0:T(8,128)(2,1)} %constant.84.clone.refs_7_.refs_8_.refs_9_.refs_10_) | copy-start | bytes 1572868
  84.4 12.4 %copy-start.25 = (bf16[2,256,256]{2,1,0:T(8,128)(2,1)S(1)}, bf16[2,256,256]{2,1,0:T(8,128)(2,1)}, u32[]{:S(2)}) copy-start(bf16[2,256,256]{2,1,0:T(8,128)(2,1)} %constant.81.clone.refs_4_.refs_5_.refs_6_.refs_7_) | copy-start | bytes 786436
  94.1 22.3 %collective-permute-start.9 = (f32[2,4,256,128]{3,2,1,0:T(8,128)}, f32[2,4,256,128]{3,2,1,0:T(8,128)}, u32[]{:S(2)}, u32[]{:S(2)}) collective-permute-start(f32[2,4,256,128]{3,2,1,0:T(8,128)} %get-tuple-element.57), channel_id=1, source_target_pairs={{0,4},{4,8},{8,12},{12,16},{16,20},{20,24},{24,28},{28,32},{32,36}... | collective-permute-start | bytes 3145736 | tf_op jit(solution)/shard_map/grad_2/ppermute | solution.py:344
  96.8 7.1 %copy-start.28 = (bf16[2,256,256]{2,1,0:T(8,128)(2,1)S(1)}, bf16[2,256,256]{2,1,0:T(8,128)(2,1)}, u32[]{:S(2)}) copy-start(bf16[2,256,256]{2,1,0:T(8,128)(2,1)} %constant.83.clone.refs_6_.refs_7_.refs_8_.refs_9_) | copy-start | bytes 786436
  110.2 1.8 copy-start.11
  110.2 101.2 %copy-start.2 = (f32[2,4,256,128]{3,2,1,0:T(8,128)S(1)}, f32[2,4,256,128]{3,2,1,0:T(8,128)}, u32[]{:S(2)}) copy-start(f32[2,4,256,128]{3,2,1,0:T(8,128)} %copy-done.1) | copy-start | bytes 3145732
  112.1 2.3 collective-permute-start.8
  116.4 54.6 %collective-permute-start.13 = (f32[2,2,256,128]{3,2,1,0:T(8,128)}, f32[2,2,256,128]{3,2,1,0:T(8,128)}, u32[]{:S(2)}, u32[]{:S(2)}) collective-permute-start(f32[2,2,256,128]{3,2,1,0:T(8,128)} %copy-done.13), channel_id=1, source_target_pairs={{0,4},{4,8},{8,12},{12,16},{16,20},{20,24},{24,28},{28,32},{32,36}... | collective-permute-start | bytes 1572872 | tf_op jit(solution)/shard_map/grad_3/ppermute | solution.py:344
  129.9 31.1 %collective-permute-start.10 = (f32[128,256]{1,0:T(8,128)}, f32[128,256]{1,0:T(8,128)}, u32[]{:S(2)}, u32[]{:S(2)}) collective-permute-start(f32[128,256]{1,0:T(8,128)} %get-tuple-element.88), channel_id=1, source_target_pairs={{0,2},{1,3},{2,0},{3,1},{4,6},{5,7},{6,4},{7,5},{8,10},{9,11},{10,... | collective-permute-start | bytes 393224 | tf_op jit(solution)/shard_map/swap_y1/ppermute | solution.py:373
  137.3 30.3 %collective-permute-start.11 = (f32[128,256]{1,0:T(8,128)}, f32[128,256]{1,0:T(8,128)}, u32[]{:S(2)}, u32[]{:S(2)}) collective-permute-start(f32[128,256]{1,0:T(8,128)} %get-tuple-element.87), channel_id=1, source_target_pairs={{0,64},{1,65},{2,66},{3,67},{4,68},{5,69},{6,70},{7,71},{8,72},{9,... | collective-permute-start | bytes 393224 | tf_op jit(solution)/shard_map/swap_y2/ppermute | solution.py:373
  161.0 9.0 %collective-permute-start.12 = (f32[128,256]{1,0:T(8,128)S(1)}, f32[128,256]{1,0:T(8,128)}, u32[]{:S(2)}, u32[]{:S(2)}) collective-permute-start(f32[128,256]{1,0:T(8,128)S(1)} %get-tuple-element.86), channel_id=1, source_target_pairs={{0,66},{1,67},{2,64},{3,65},{4,70},{5,71},{6,68},{7,69},{8,74},{9,... | collective-permute-start | bytes 393224 | tf_op jit(solution)/shard_map/swap_y3/ppermute | solution.py:373
  171.1 25.8 %collective-permute-start.20 = (f32[2,3,256,128]{3,2,1,0:T(8,128)}, f32[2,3,256,128]{3,2,1,0:T(8,128)S(1)}, u32[]{:S(2)}, u32[]{:S(2)}) collective-permute-start(f32[2,3,256,128]{3,2,1,0:T(8,128)} %copy-done.11), channel_id=1, source_target_pairs={{0,4},{4,8},{8,12},{12,16},{16,20},{20,24},{24,28},{28,32},{32,36}... | collective-permute-start | bytes 2359304 | tf_op jit(solution)/shard_map/grad_4/ppermute | solution.py:344
  172.4 14.0 %collective-permute-start.15 = (f32[128,256]{1,0:T(8,128)S(1)}, f32[128,256]{1,0:T(8,128)S(1)}, u32[]{:S(2)}, u32[]{:S(2)}) collective-permute-start(f32[128,256]{1,0:T(8,128)S(1)} %fusion), channel_id=1, source_target_pairs={{0,32},{1,33},{2,34},{3,35},{4,36},{5,37},{6,38},{7,39},{8,40},{9,... | collective-permute-start | bytes 393224 | tf_op jit(solution)/shard_map/swap_z2/ppermute | solution.py:373
  172.5 13.9 %collective-permute-start.16 = (f32[128,256]{1,0:T(8,128)S(1)}, f32[128,256]{1,0:T(8,128)S(1)}, u32[]{:S(2)}, u32[]{:S(2)}) collective-permute-start(f32[128,256]{1,0:T(8,128)S(1)} %fusion), channel_id=1, source_target_pairs={{0,48},{1,49},{2,50},{3,51},{4,52},{5,53},{6,54},{7,55},{8,56},{9,... | collective-permute-start | bytes 393224 | tf_op jit(solution)/shard_map/swap_z3/ppermute | solution.py:373
  172.6 14.7 %collective-permute-start.14 = (f32[128,256]{1,0:T(8,128)S(1)}, f32[128,256]{1,0:T(8,128)S(1)}, u32[]{:S(2)}, u32[]{:S(2)}) collective-permute-start(f32[128,256]{1,0:T(8,128)S(1)} %fusion), channel_id=1, source_target_pairs={{0,16},{1,17},{2,18},{3,19},{4,20},{5,21},{6,22},{7,23},{8,24},{9,... | collective-permute-start | bytes 393224 | tf_op jit(solution)/shard_map/swap_z1/ppermute | solution.py:373
  187.4 6.2 %collective-permute-start.18 = (f32[128,256]{1,0:T(8,128)S(1)}, f32[128,256]{1,0:T(8,128)S(1)}, u32[]{:S(2)}, u32[]{:S(2)}) collective-permute-start(f32[128,256]{1,0:T(8,128)S(1)} %add_add_fusion), channel_id=1, source_target_pairs={{0,8},{1,9},{2,10},{3,11},{4,12},{5,13},{6,14},{7,15},{8,0},{9,1},... | collective-permute-start | bytes 393224 | tf_op jit(solution)/shard_map/swap_x2/ppermute | solution.py:373
  187.5 9.3 %collective-permute-start.19 = (f32[128,256]{1,0:T(8,128)S(1)}, f32[128,256]{1,0:T(8,128)S(1)}, u32[]{:S(2)}, u32[]{:S(2)}) collective-permute-start(f32[128,256]{1,0:T(8,128)S(1)} %add_add_fusion), channel_id=1, source_target_pairs={{0,12},{1,13},{2,14},{3,15},{4,8},{5,9},{6,10},{7,11},{8,4},{9,5},... | collective-permute-start | bytes 393224 | tf_op jit(solution)/shard_map/swap_x3/ppermute | solution.py:373
  188.2 8.6 %collective-permute-start.17 = (f32[128,256]{1,0:T(8,128)S(1)}, f32[128,256]{1,0:T(8,128)S(1)}, u32[]{:S(2)}, u32[]{:S(2)}) collective-permute-start(f32[128,256]{1,0:T(8,128)S(1)} %add_add_fusion), channel_id=1, source_target_pairs={{0,4},{1,5},{2,6},{3,7},{4,0},{5,1},{6,2},{7,3},{8,12},{9,13},{10,... | collective-permute-start | bytes 393224 | tf_op jit(solution)/shard_map/swap_x1/ppermute | solution.py:373
  197.7 25.7 %collective-permute-start.25 = (f32[2,2,256,128]{3,2,1,0:T(8,128)}, f32[2,2,256,128]{3,2,1,0:T(8,128)}, u32[]{:S(2)}, u32[]{:S(2)}) collective-permute-start(f32[2,2,256,128]{3,2,1,0:T(8,128)} %copy-done.12), channel_id=1, source_target_pairs={{0,5},{1,6},{2,7},{4,9},{5,10},{6,11},{8,13},{9,14},{10,15},{12,17... | collective-permute-start | bytes 1572872 | tf_op jit(solution)/shard_map/slant/ppermute | solution.py:353
  202.1 20.2 %collective-permute-start.23 = (f32[128,256]{1,0:T(8,128)S(1)}, f32[128,256]{1,0:T(8,128)}, u32[]{:S(2)}, u32[]{:S(2)}) collective-permute-start(f32[128,256]{1,0:T(8,128)S(1)} %add_multiply_fusion), channel_id=1, source_target_pairs={{0,64},{1,65},{2,66},{3,67},{4,68},{5,69},{6,70},{7,71},{8,72},{9,... | collective-permute-start | bytes 393224 | tf_op jit(solution)/shard_map/swap_y2/ppermute | solution.py:373
  211.5 10.8 %collective-permute-start.24 = (f32[128,256]{1,0:T(8,128)S(1)}, f32[128,256]{1,0:T(8,128)}, u32[]{:S(2)}, u32[]{:S(2)}) collective-permute-start(f32[128,256]{1,0:T(8,128)S(1)} %add_multiply_fusion), channel_id=1, source_target_pairs={{0,66},{1,67},{2,64},{3,65},{4,70},{5,71},{6,68},{7,69},{8,74},{9,... | collective-permute-start | bytes 393224 | tf_op jit(solution)/shard_map/swap_y3/ppermute | solution.py:373
  211.5 10.8 %collective-permute-start.22 = (f32[128,256]{1,0:T(8,128)S(1)}, f32[128,256]{1,0:T(8,128)}, u32[]{:S(2)}, u32[]{:S(2)}) collective-permute-start(f32[128,256]{1,0:T(8,128)S(1)} %add_multiply_fusion), channel_id=1, source_target_pairs={{0,2},{1,3},{2,0},{3,1},{4,6},{5,7},{6,4},{7,5},{8,10},{9,11},{10,... | collective-permute-start | bytes 393224 | tf_op jit(solution)/shard_map/swap_y1/ppermute | solution.py:373
  211.5 1.2 copy-start.4
  217.1 11.6 %collective-permute-start.21 = (f32[2,2,256,128]{3,2,1,0:T(8,128)}, f32[2,2,256,128]{3,2,1,0:T(8,128)S(1)}, u32[]{:S(2)}, u32[]{:S(2)}) collective-permute-start(f32[2,2,256,128]{3,2,1,0:T(8,128)} %get-tuple-element.67), channel_id=1, source_target_pairs={{0,1},{1,2},{2,3},{4,5},{5,6},{6,7},{8,9},{9,10},{10,11},{12,13},{... | collective-permute-start | bytes 1572872 | tf_op jit(solution)/shard_map/over/ppermute | solution.py:344
  223.5 8.6 %collective-permute-start.26 = (f32[512,256]{1,0:T(8,128)S(1)}, f32[512,256]{1,0:T(8,128)}, u32[]{:S(2)}, u32[]{:S(2)}) collective-permute-start(f32[512,256]{1,0:T(8,128)S(1)} %pad_maximum_fusion.2), channel_id=1, source_target_pairs={{0,1},{1,0},{2,3},{3,2},{4,5},{5,4},{6,7},{7,6},{8,9},{9,8},{10,11... | collective-permute-start | bytes 1572872 | tf_op jit(solution)/shard_map/swap_c1/ppermute | solution.py:373
  228.7 1.1 copy-start.6
  (17 other events, 16.1 us)

commit v2 on v0

--- a/solution.py
+++ b/solution.py
@@ -454,13 +454,14 @@
     v, _ = exchanged_sum(v, 2)
     sources = [(first, array) for (first, _), pair in zip(plan, zip(uppers, comings)) for array in pair]
     step = finish(range(2, 13), sources[:8], field.shape, None)
-    v, comings[4], step, over_upper = tie((v, comings[4], step, over_upper))
+    v, comings[4], over_upper = tie((v, comings[4], over_upper))
     over = shifted(over_upper, "mode", 1, "over")
     v, _ = exchanged_sum(v, 3)
     slots_all = lax.axis_size("scan") * lax.axis_size("mode") * SLOTS
     v = v * (1.0 / math.sqrt(slots_all))
     v, slant = tie((v, slant))
     v = gathered(v, 1, y, 4)
+    v, step = tie((v, step))
     probe_step = gathered(v, 0, core, 2).reshape(probe.shape)
     sources = sources[:2] + [(13, uppers[4]), (13, comings[4]), (0, over), (0, slant)]
     step = finish([0, 1, 13, 14, 15], sources, field.shape, step)

time: 228 us -> 234 us (1.026)
  the two profiles are of different devices: /device:TPU:72 before, /device:TPU:1 now
where the time goes in v2:
time: 234 us; the launch traced here: 233 us
  starting transfers between devices  93.7 us (40%)
  waiting for transfers between devices  58.6 us (25%)
  Pallas kernels  37.9 us (16%)
  local copies, waits for them, and re-layouts  34.6 us (15%)
  other arithmetic  6.87 us (3%)
    ppermute x14, starting transfers between devices, swapped(): return lax.ppermute(array, AXES, pairs)  44.7 us
    ppermute x12, starting transfers between devices, shifted(): return lax.ppermute(array, axis, pairs)  44.2 us
    ppermute x12, waiting for transfers between devices, shifted(): return lax.ppermute(array, axis, pairs)  35.5 us
    pallas_call x5, Pallas kernels, run_group(): pl.pallas_call(functools.partial(group_kernel, first, count, (homes[0], h...  32.2 us
    ppermute x14, waiting for transfers between devices, swapped(): return lax.ppermute(array, AXES, pairs)  23 us
    unnamed x75, local copies, waits for them, and re-layouts  22.8 us
    pallas_call x2, Pallas kernels, finish(): pl.pallas_call(functools.partial(finish_kernel, tuple(blocks), terms), ou...  5.63 us
    ppermute x1, starting transfers between devices, shifted_both(): return lax.ppermute(array, AXES, pairs)  4.81 us
  transfers between devices with their start and end apart: 27, of which 9 were waited for; matrix products, arithmetic and copies ran while one was open for 6% of the time, Pallas kernels for 16%

profile of v2, /device:TPU:1, one launch (start us, length us, event | category | flops | bytes accessed | tf_op | source)
XLA Modules:
  0.0 233.5 jit_solution(13198572254856007142)
XLA Ops:
  0.6 2.5 %slice.21 = f32[2,256,640]{2,1,0:T(8,128)} slice(f32[2,256,2048]{2,1,0:T(8,128)} %refs_0_.9), slice={[0:2], [0:256], [0:640]} | slice | bytes 2621440 | tf_op jit(solution)/shard_map/slice | solution.py:420
  3.2 1.3 collective-permute-start
  4.5 3.0 %fusion.1 = (f32[2,256,512]{2,1,0:T(8,128)}, f32[2,256,512]{2,1,0:T(8,128)}) fusion(f32[2,256,2048]{2,1,0:T(8,128)} %refs_0_.9), kind=kLoop, calls=%fused_computation.20 | loop fusion | bytes 4194304 | tf_op jit(solution)/shard_map/slice | solution.py:423
  7.5 1.3 collective-permute-start.6
  9.7 1.6 reshape.17
  11.3 1.3 copy.13
  12.6 22.7 %collective-permute-done.refs_1_ = f32[2,256,640]{2,1,0:T(8,128)S(1)} collective-permute-done((f32[2,256,640]{2,1,0:T(8,128)}, f32[2,256,640]{2,1,0:T(8,128)S(1)}, u32[]{:S(2)}, u32[]{:S(2)}) %collective-permute-start) | collective-permute-done | bytes 1310752 | tf_op jit(solution)/shard_map/halo_0/ppermute | solution.py:344
  36.5 1.3 copy-done.10
  37.8 1.0 copy-done.14
  38.8 1.0 copy-done.18
  40.9 6.3 %group_0.1 = (f32[2,3,256,128]{3,2,1,0:T(8,128)S(1)}, f32[2,3,256,128]{3,2,1,0:T(8,128)S(1)}, f32[2,2,512,128]{3,2,1,0:T(8,128)S(1)}, f32[2,2,256,256]{3,2,1,0:T(8,128)S(1)}) custom-call(s32[1]{0:T(128)S(6)} %copy.15.live, s32[16,2]{1,0:T(8,128)S(1)} %broadcast_subtract_fusion.off, f32[2,256,2048]{2,1,0:T(8,128)} %refs_0_.9, f32[2,256,640]{2,1,0:T(8,128)S(1)} %copy-done.10, ...), custom_call_target="tpu_custom_call" | custom-call | flops 8589934592 | bytes 4096 | tf_op jit(solution)/shard_map/group_0/pallas_call | solution.py:271
  47.2 1.3 collective-permute-start.1
  48.5 1.3 collective-permute-start.5
  50.9 7.1 %collective-permute-start.4 = (f32[2,512,256]{2,1,0:T(8,128)}, f32[2,512,256]{2,1,0:T(8,128)}, u32[]{:S(2)}, u32[]{:S(2)}) collective-permute-start(f32[2,512,256]{2,1,0:T(8,128)} %pad_maximum_fusion), channel_id=1, source_target_pairs={{1,0},{2,1},{3,2},{5,4},{6,5},{7,6},{9,8},{10,9},{11,10},{13,12},{... | collective-permute-start | bytes 3145736 | tf_op jit(solution)/shard_map/corner/ppermute | solution.py:344
  58.1 2.4 %group_3.1 = (f32[2,4,256,128]{3,2,1,0:T(8,128)S(1)}, f32[2,4,256,128]{3,2,1,0:T(8,128)}, f32[2,2,512,128]{3,2,1,0:T(8,128)S(1)}, f32[2,2,256,256]{3,2,1,0:T(8,128)S(1)}) custom-call(s32[1]{0:T(128)S(6)} %copy.15.live, s32[16,2]{1,0:T(8,128)S(1)} %broadcast_subtract_fusion.off, f32[2,256,2048]{2,1,0:T(8,128)} %refs_0_.9, f32[2,256,640]{2,1,0:T(8,128)} %copy-done.9, ...), custom_call_target="tpu_custom_call" | custom-call | flops 8589934592 | bytes 4096 | tf_op jit(solution)/shard_map/group_3/pallas_call | solution.py:271
  63.4 5.2 %collective-permute-start.7 = (f32[2,4,256,128]{3,2,1,0:T(8,128)}, f32[2,4,256,128]{3,2,1,0:T(8,128)}, u32[]{:S(2)}, u32[]{:S(2)}) collective-permute-start(f32[2,4,256,128]{3,2,1,0:T(8,128)} %get-tuple-element.48), channel_id=1, source_target_pairs={{0,4},{4,8},{8,12},{12,16},{16,20},{20,24},{24,28},{28,32},{32,36}... | collective-permute-start | bytes 3145736 | tf_op jit(solution)/shard_map/grad_1/ppermute | solution.py:344
  69.4 1.3 collective-permute-start.2
  71.4 1.3 collective-permute-start.3
  72.7 7.7 %collective-permute-done.5.refs_2_.refs_1_ = f32[2,256,512]{2,1,0:T(8,128)} collective-permute-done((f32[2,256,512]{2,1,0:T(8,128)}, f32[2,256,512]{2,1,0:T(8,128)}, u32[]{:S(2)}, u32[]{:S(2)}) %collective-permute-start.5) | collective-permute-done | bytes 1048608 | tf_op jit(solution)/shard_map/halo_2/ppermute | solution.py:344
  80.4 1.0 copy-done.16
  81.4 1.0 copy-done.20
  84.4 10.7 %group_7.1 = (f32[2,4,256,128]{3,2,1,0:T(8,128)S(1)}, f32[2,4,256,128]{3,2,1,0:T(8,128)}, f32[2,2,512,128]{3,2,1,0:T(8,128)S(1)}, f32[2,2,256,256]{3,2,1,0:T(8,128)S(1)}) custom-call(s32[1]{0:T(128)S(6)} %copy.15.live, s32[16,2]{1,0:T(8,128)S(1)} %broadcast_subtract_fusion.off, f32[2,256,2048]{2,1,0:T(8,128)} %refs_0_.9, ...), custom_call_target="tpu_custom_call" | custom-call | flops 8589934592 | bytes 4096 | tf_op jit(solution)/shard_map/group_7/pallas_call | solution.py:271
  98.0 2.3 collective-permute-start.9
  100.3 5.5 %group_11.1 = (f32[2,2,256,128]{3,2,1,0:T(8,128)S(1)}, f32[2,2,256,128]{3,2,1,0:T(8,128)S(1)}, f32[2,2,512,128]{3,2,1,0:T(8,128)S(1)}, f32[2,2,256,256]{3,2,1,0:T(8,128)S(1)}) custom-call(s32[1]{0:T(128)S(6)} %copy.15.live, s32[16,2]{1,0:T(8,128)S(1)} %broadcast_subtract_fusion.off, f32[2,256,2048]{2,1,0:T(8,128)} %refs_0_.9, ...), custom_call_target="tpu_custom_call" | custom-call | flops 8589934592 | bytes 4096 | tf_op jit(solution)/shard_map/group_11/pallas_call | solution.py:271
  107.4 7.4 %group_13.1 = (f32[2,3,256,128]{3,2,1,0:T(8,128)S(1)}, f32[2,3,256,128]{3,2,1,0:T(8,128)S(1)}, f32[2,2,256,128]{3,2,1,0:T(8,128)}, f32[2,2,256,128]{3,2,1,0:T(8,128)S(1)}, f32[2,2,256,256]{3,2,1,0:T(8,128)S(1)}) custom-call(s32[1]{0:T(128)S(6)} %copy.15.live, s32[16,2]{1,0:T(8,128)S(1)} %broadcast_subtract_fusion.off, f32[2,256,2048]{2,1,0:T(8,128)} %refs_0_.9, ...), custom_call_target="tpu_custom_call" | custom-call | flops 8589934592 | bytes 4096 | tf_op jit(solution)/shard_map/group_13/pallas_call | solution.py:271
  117.5 7.8 %collective-permute-start.13 = (f32[2,2,256,128]{3,2,1,0:T(8,128)}, f32[2,2,256,128]{3,2,1,0:T(8,128)}, u32[]{:S(2)}, u32[]{:S(2)}) collective-permute-start(f32[2,2,256,128]{3,2,1,0:T(8,128)} %copy-done.13), channel_id=1, source_target_pairs={{0,4},{4,8},{8,12},{12,16},{16,20},{20,24},{24,28},{28,32},{32,36}... | collective-permute-start | bytes 1572872 | tf_op jit(solution)/shard_map/grad_3/ppermute | solution.py:344
  125.3 1.3 bitcast_add_fusion
  126.6 9.6 %collective-permute-start.17 = (f32[2,3,256,128]{3,2,1,0:T(8,128)}, f32[2,3,256,128]{3,2,1,0:T(8,128)}, u32[]{:S(2)}, u32[]{:S(2)}) collective-permute-start(f32[2,3,256,128]{3,2,1,0:T(8,128)} %copy-done.11), channel_id=1, source_target_pairs={{0,4},{4,8},{8,12},{12,16},{16,20},{20,24},{24,28},{28,32},{32,36}... | collective-permute-start | bytes 2359304 | tf_op jit(solution)/shard_map/grad_4/ppermute | solution.py:344
  136.9 21.8 %collective-permute-start.11 = (f32[128,256]{1,0:T(8,128)}, f32[128,256]{1,0:T(8,128)}, u32[]{:S(2)}, u32[]{:S(2)}) collective-permute-start(f32[128,256]{1,0:T(8,128)} %get-tuple-element.87), channel_id=1, source_target_pairs={{0,64},{1,65},{2,66},{3,67},{4,68},{5,69},{6,70},{7,71},{8,72},{9,... | collective-permute-start | bytes 393224 | tf_op jit(solution)/shard_map/swap_y2/ppermute | solution.py:373
  158.9 6.3 %collective-permute-done.11 = f32[128,256]{1,0:T(8,128)} collective-permute-done((f32[128,256]{1,0:T(8,128)}, f32[128,256]{1,0:T(8,128)}, u32[]{:S(2)}, u32[]{:S(2)}) %collective-permute-start.11) | collective-permute-done | bytes 131104 | tf_op jit(solution)/shard_map/swap_y2/ppermute | solution.py:373
  165.3 2.3 collective-permute-done.12
  167.6 1.1 fusion
  168.8 6.7 %collective-permute-start.16 = (f32[128,256]{1,0:T(8,128)S(1)}, f32[128,256]{1,0:T(8,128)S(1)}, u32[]{:S(2)}, u32[]{:S(2)}) collective-permute-start(f32[128,256]{1,0:T(8,128)S(1)} %fusion), channel_id=1, source_target_pairs={{0,48},{1,49},{2,50},{3,51},{4,52},{5,53},{6,54},{7,55},{8,56},{9,... | collective-permute-start | bytes 393224 | tf_op jit(solution)/shard_map/swap_z3/ppermute | solution.py:373
  176.0 4.8 %collective-permute-start.22 = (f32[2,2,256,128]{3,2,1,0:T(8,128)}, f32[2,2,256,128]{3,2,1,0:T(8,128)S(1)}, u32[]{:S(2)}, u32[]{:S(2)}) collective-permute-start(f32[2,2,256,128]{3,2,1,0:T(8,128)} %copy-done.12), channel_id=1, source_target_pairs={{0,5},{1,6},{2,7},{4,9},{5,10},{6,11},{8,13},{9,14},{10,15},{12,17... | collective-permute-start | bytes 1572872 | tf_op jit(solution)/shard_map/slant/ppermute | solution.py:353
  182.0 3.0 %collective-permute-start.20 = (f32[128,256]{1,0:T(8,128)S(1)}, f32[128,256]{1,0:T(8,128)S(1)}, u32[]{:S(2)}, u32[]{:S(2)}) collective-permute-start(f32[128,256]{1,0:T(8,128)S(1)} %add_add_fusion), channel_id=1, source_target_pairs={{0,8},{1,9},{2,10},{3,11},{4,12},{5,13},{6,14},{7,15},{8,0},{9,1},... | collective-permute-start | bytes 393224 | tf_op jit(solution)/shard_map/swap_x2/ppermute | solution.py:373
  184.9 1.6 collective-permute-start.21
  186.5 9.9 %collective-permute-done.20 = f32[128,256]{1,0:T(8,128)S(1)} collective-permute-done((f32[128,256]{1,0:T(8,128)S(1)}, f32[128,256]{1,0:T(8,128)S(1)}, u32[]{:S(2)}, u32[]{:S(2)}) %collective-permute-start.20) | collective-permute-done | bytes 131104 | tf_op jit(solution)/shard_map/swap_x2/ppermute | solution.py:373
  196.5 3.4 %collective-permute-done.21 = f32[128,256]{1,0:T(8,128)S(1)} collective-permute-done((f32[128,256]{1,0:T(8,128)S(1)}, f32[128,256]{1,0:T(8,128)S(1)}, u32[]{:S(2)}, u32[]{:S(2)}) %collective-permute-start.21) | collective-permute-done | bytes 131104 | tf_op jit(solution)/shard_map/swap_x3/ppermute | solution.py:373
  200.7 10.7 %collective-permute-start.24 = (f32[128,256]{1,0:T(8,128)S(1)}, f32[128,256]{1,0:T(8,128)}, u32[]{:S(2)}, u32[]{:S(2)}) collective-permute-start(f32[128,256]{1,0:T(8,128)S(1)} %add_multiply_fusion), channel_id=1, source_target_pairs={{0,64},{1,65},{2,66},{3,67},{4,68},{5,69},{6,70},{7,71},{8,72},{9,... | collective-permute-start | bytes 393224 | tf_op jit(solution)/shard_map/swap_y2/ppermute | solution.py:373
  211.4 1.2 copy-done.4
  212.6 1.0 copy-done.8
  213.7 3.4 %finish_2.1.refs_6_ = f32[2,256,2048]{2,1,0:T(8,128)} custom-call(f32[2,3,256,128]{3,2,1,0:T(8,128)S(1)} %get-tuple-element.43.refs_0_, f32[2,3,256,128]{3,2,1,0:T(8,128)S(1)} %collective-permute-done.1.refs_3_.refs_1_, f32[2,4,256,128]{3,2,1,0:T(8,128)S(1)} %copy-done.2, f32[2,4,256,128]{3,2,1,0:T(8,128)} %collective-permute-done.7.refs_3_, ...), custom_call_target="tpu_custom_call" | custom-call | tf_op jit(solution)/shard_map/finish_2/pallas_call | solution.py:325
  217.0 4.5 %collective-permute-start.18 = (f32[2,2,256,128]{3,2,1,0:T(8,128)}, f32[2,2,256,128]{3,2,1,0:T(8,128)S(1)}, u32[]{:S(2)}, u32[]{:S(2)}) collective-permute-start(f32[2,2,256,128]{3,2,1,0:T(8,128)} %get-tuple-element.66), channel_id=1, source_target_pairs={{0,1},{1,2},{2,3},{4,5},{5,6},{6,7},{8,9},{9,10},{10,11},{12,13},{... | collective-permute-start | bytes 1572872 | tf_op jit(solution)/shard_map/over/ppermute | solution.py:344
  221.6 1.1 select_select_fusion.3
  222.8 5.1 %collective-permute-done.18.refs_4_ = f32[2,2,256,128]{3,2,1,0:T(8,128)S(1)} collective-permute-done((f32[2,2,256,128]{3,2,1,0:T(8,128)}, f32[2,2,256,128]{3,2,1,0:T(8,128)S(1)}, u32[]{:S(2)}, u32[]{:S(2)}) %collective-permute-start.18) | collective-permute-done | bytes 524320 | tf_op jit(solution)/shard_map/over/ppermute | solution.py:344
  228.0 1.0 copy-done.6
  229.0 2.3 finish_0.1
  231.3 1.1 broadcast_select_fusion.1
  (113 shorter events, 21.7 us)
Async XLA Ops:
  0.6 8.2 %copy-start.36 = (s32[16,2]{0,1:T(2,128)S(1)}, s32[16,2]{0,1:T(2,128)}, u32[]{:S(2)}) copy-start(s32[16,2]{0,1:T(2,128)} %param.12) | copy-start | bytes 388
  0.6 9.0 %copy-start.35 = (f32[2,2,256,256]{3,2,1,0:T(8,128)S(1)}, f32[2,2,256,256]{3,2,1,0:T(8,128)}, u32[]{:S(2)}) copy-start(f32[2,2,256,256]{3,2,1,0:T(8,128)} %param.10) | copy-start | bytes 3145732
  3.2 32.1 %collective-permute-start = (f32[2,256,640]{2,1,0:T(8,128)}, f32[2,256,640]{2,1,0:T(8,128)S(1)}, u32[]{:S(2)}, u32[]{:S(2)}) collective-permute-start(f32[2,256,640]{2,1,0:T(8,128)} %slice.21), channel_id=1, source_target_pairs={{4,0},{8,4},{12,8},{16,12},{20,16},{24,20},{28,24},{32,28},{36,32}... | collective-permute-start | bytes 3932168 | tf_op jit(solution)/shard_map/halo_0/ppermute | solution.py:344
  7.5 50.5 %collective-permute-start.6 = (f32[2,256,512]{2,1,0:T(8,128)}, f32[2,256,512]{2,1,0:T(8,128)}, u32[]{:S(2)}, u32[]{:S(2)}) collective-permute-start(f32[2,256,512]{2,1,0:T(8,128)} %get-tuple-element.78), channel_id=1, source_target_pairs={{4,0},{8,4},{12,8},{16,12},{20,16},{24,20},{28,24},{32,28},{36,32}... | collective-permute-start | bytes 3145736 | tf_op jit(solution)/shard_map/halo_1/ppermute | solution.py:344
  9.0 27.5 %copy-start.22 = (bf16[2,256,256]{2,1,0:T(8,128)(2,1)S(1)}, bf16[2,256,256]{2,1,0:T(8,128)(2,1)}, u32[]{:S(2)}) copy-start(bf16[2,256,256]{2,1,0:T(8,128)(2,1)} %constant.81.clone.refs_4_.refs_5_.refs_6_.refs_7_) | copy-start | bytes 786436
  35.3 1.1 copy-start.9
  36.5 1.3 copy-start.10
  37.8 1.0 copy-start.14
  40.8 9.0 %slice-start = ((f32[2,256,640]{2,1,0:T(8,128)}), f32[2,256,256]{2,1,0:T(8,128)S(1)}, s32[]{:S(2)}) async-start(f32[2,256,640]{2,1,0:T(8,128)} %copy-done.9), calls=%async_computation | async-start | bytes 1048576 | tf_op jit(solution)/shard_map/slice | solution.py:427
  40.8 9.0 %slice-start.1 = ((f32[2,256,2048]{2,1,0:T(8,128)}), f32[2,256,256]{2,1,0:T(8,128)S(1)}, s32[]{:S(2)}) async-start(f32[2,256,2048]{2,1,0:T(8,128)} %refs_0_.9), calls=%async_computation.1 | async-start | bytes 1048576 | tf_op jit(solution)/shard_map/slice | solution.py:427
  40.8 17.2 %copy-start.15 = (bf16[512,512]{1,0:T(8,128)(2,1)S(1)}, bf16[512,512]{1,0:T(8,128)(2,1)}, u32[]{:S(2)}) copy-start(bf16[512,512]{1,0:T(8,128)(2,1)} %constant.82.clone.refs_5_.refs_6_.refs_7_.refs_8_) | copy-start | bytes 1572868
  40.8 17.2 %copy-start.19 = (bf16[512,512]{1,0:T(8,128)(2,1)S(1)}, bf16[512,512]{1,0:T(8,128)(2,1)}, u32[]{:S(2)}) copy-start(bf16[512,512]{1,0:T(8,128)(2,1)} %constant.84.clone.refs_7_.refs_8_.refs_9_.refs_10_) | copy-start | bytes 1572868
  40.8 17.2 %copy-start.23 = (bf16[2,256,256]{2,1,0:T(8,128)(2,1)S(1)}, bf16[2,256,256]{2,1,0:T(8,128)(2,1)}, u32[]{:S(2)}) copy-start(bf16[2,256,256]{2,1,0:T(8,128)(2,1)} %constant.81.clone.refs_4_.refs_5_.refs_6_.refs_7_) | copy-start | bytes 786436
  47.2 24.3 %collective-permute-start.1 = (f32[2,3,256,128]{3,2,1,0:T(8,128)S(1)}, f32[2,3,256,128]{3,2,1,0:T(8,128)S(1)}, u32[]{:S(2)}, u32[]{:S(2)}) collective-permute-start(f32[2,3,256,128]{3,2,1,0:T(8,128)S(1)} %get-tuple-element.44), channel_id=1, source_target_pairs={{0,4},{4,8},{8,12},{12,16},{16,20},{20,24},{24,28},{28,32},{32,36}... | collective-permute-start | bytes 2359304 | tf_op jit(solution)/shard_map/grad_0/ppermute | solution.py:344
  48.5 31.9 %collective-permute-start.5 = (f32[2,256,512]{2,1,0:T(8,128)}, f32[2,256,512]{2,1,0:T(8,128)}, u32[]{:S(2)}, u32[]{:S(2)}) collective-permute-start(f32[2,256,512]{2,1,0:T(8,128)} %get-tuple-element.45), channel_id=1, source_target_pairs={{4,0},{8,4},{12,8},{16,12},{20,16},{24,20},{28,24},{32,28},{36,32}... | collective-permute-start | bytes 3145736 | tf_op jit(solution)/shard_map/halo_2/ppermute | solution.py:344
  50.9 49.4 %collective-permute-start.4 = (f32[2,512,256]{2,1,0:T(8,128)}, f32[2,512,256]{2,1,0:T(8,128)}, u32[]{:S(2)}, u32[]{:S(2)}) collective-permute-start(f32[2,512,256]{2,1,0:T(8,128)} %pad_maximum_fusion), channel_id=1, source_target_pairs={{1,0},{2,1},{3,2},{5,4},{6,5},{7,6},{9,8},{10,9},{11,10},{13,12},{... | collective-permute-start | bytes 3145736 | tf_op jit(solution)/shard_map/corner/ppermute | solution.py:344
  58.1 10.5 %copy-start.33 = (f32[2,256,2048]{2,1,0:T(8,128)S(1)}, f32[2,256,2048]{2,1,0:T(8,128)}, u32[]{:S(2)}) copy-start(f32[2,256,2048]{2,1,0:T(8,128)} %refs_0_.9) | copy-start | bytes 12582916
  63.4 36.9 %collective-permute-start.7 = (f32[2,4,256,128]{3,2,1,0:T(8,128)}, f32[2,4,256,128]{3,2,1,0:T(8,128)}, u32[]{:S(2)}, u32[]{:S(2)}) collective-permute-start(f32[2,4,256,128]{3,2,1,0:T(8,128)} %get-tuple-element.48), channel_id=1, source_target_pairs={{0,4},{4,8},{8,12},{12,16},{16,20},{20,24},{24,28},{28,32},{32,36}... | collective-permute-start | bytes 3145736 | tf_op jit(solution)/shard_map/grad_1/ppermute | solution.py:344
  69.4 30.8 %collective-permute-start.2 = (f32[2,256,256]{2,1,0:T(8,128)}, f32[2,256,256]{2,1,0:T(8,128)}, u32[]{:S(2)}, u32[]{:S(2)}) collective-permute-start(f32[2,256,256]{2,1,0:T(8,128)} %slice.23), channel_id=1, source_target_pairs={{4,0},{8,4},{12,8},{16,12},{20,16},{24,20},{28,24},{32,28},{36,32}... | collective-permute-start | bytes 1572872 | tf_op jit(solution)/shard_map/halo_3/ppermute | solution.py:344
  71.4 36.0 %collective-permute-start.3 = (f32[2,256,128]{2,1,0:T(8,128)}, f32[2,256,128]{2,1,0:T(8,128)S(1)}, u32[]{:S(2)}, u32[]{:S(2)}) collective-permute-start(f32[2,256,128]{2,1,0:T(8,128)} %slice.24), channel_id=1, source_target_pairs={{4,0},{8,4},{12,8},{16,12},{20,16},{24,20},{28,24},{32,28},{36,32}... | collective-permute-start | bytes 786440 | tf_op jit(solution)/shard_map/halo_4/ppermute | solution.py:344
  80.4 1.0 copy-start.16
  84.4 15.9 %copy-start.17 = (bf16[512,512]{1,0:T(8,128)(2,1)S(1)}, bf16[512,512]{1,0:T(8,128)(2,1)}, u32[]{:S(2)}) copy-start(bf16[512,512]{1,0:T(8,128)(2,1)} %constant.82.clone.refs_5_.refs_6_.refs_7_.refs_8_) | copy-start | bytes 1572868
  84.4 15.9 %copy-start.21 = (bf16[512,512]{1,0:T(8,128)(2,1)S(1)}, bf16[512,512]{1,0:T(8,128)(2,1)}, u32[]{:S(2)}) copy-start(bf16[512,512]{1,0:T(8,128)(2,1)} %constant.84.clone.refs_7_.refs_8_.refs_9_.refs_10_) | copy-start | bytes 1572868
  84.4 15.9 %copy-start.25 = (bf16[2,256,256]{2,1,0:T(8,128)(2,1)S(1)}, bf16[2,256,256]{2,1,0:T(8,128)(2,1)}, u32[]{:S(2)}) copy-start(bf16[2,256,256]{2,1,0:T(8,128)(2,1)} %constant.81.clone.refs_4_.refs_5_.refs_6_.refs_7_) | copy-start | bytes 786436
  98.0 28.6 %collective-permute-start.9 = (f32[2,4,256,128]{3,2,1,0:T(8,128)}, f32[2,4,256,128]{3,2,1,0:T(8,128)}, u32[]{:S(2)}, u32[]{:S(2)}) collective-permute-start(f32[2,4,256,128]{3,2,1,0:T(8,128)} %get-tuple-element.57), channel_id=1, source_target_pairs={{0,4},{4,8},{8,12},{12,16},{16,20},{20,24},{24,28},{28,32},{32,36}... | collective-permute-start | bytes 3145736 | tf_op jit(solution)/shard_map/grad_2/ppermute | solution.py:344
  100.3 7.2 %copy-start.28 = (bf16[2,256,256]{2,1,0:T(8,128)(2,1)S(1)}, bf16[2,256,256]{2,1,0:T(8,128)(2,1)}, u32[]{:S(2)}) copy-start(bf16[2,256,256]{2,1,0:T(8,128)(2,1)} %constant.83.clone.refs_6_.refs_7_.refs_8_.refs_9_) | copy-start | bytes 786436
  115.7 1.8 copy-start.11
  115.7 95.7 %copy-start.2 = (f32[2,4,256,128]{3,2,1,0:T(8,128)S(1)}, f32[2,4,256,128]{3,2,1,0:T(8,128)}, u32[]{:S(2)}) copy-start(f32[2,4,256,128]{3,2,1,0:T(8,128)} %copy-done.1) | copy-start | bytes 3145732
  117.5 7.8 %collective-permute-start.8 = (f32[512,256]{1,0:T(8,128)}, f32[512,256]{1,0:T(8,128)}, u32[]{:S(2)}, u32[]{:S(2)}) collective-permute-start(f32[512,256]{1,0:T(8,128)} %dynamic-slice_bitcast_fusion), channel_id=1, source_target_pairs={{0,1},{1,0},{2,3},{3,2},{4,5},{5,4},{6,7},{7,6},{8,9},{9,8},{10,11... | collective-permute-start | bytes 1572872 | tf_op jit(solution)/shard_map/swap_c1/ppermute | solution.py:373
  117.5 51.2 %collective-permute-start.13 = (f32[2,2,256,128]{3,2,1,0:T(8,128)}, f32[2,2,256,128]{3,2,1,0:T(8,128)}, u32[]{:S(2)}, u32[]{:S(2)}) collective-permute-start(f32[2,2,256,128]{3,2,1,0:T(8,128)} %copy-done.13), channel_id=1, source_target_pairs={{0,4},{4,8},{8,12},{12,16},{16,20},{20,24},{24,28},{28,32},{32,36}... | collective-permute-start | bytes 1572872 | tf_op jit(solution)/shard_map/grad_3/ppermute | solution.py:344
  126.5 9.6 %copy-start.34 = (f32[512,256]{1,0:T(8,128)}, f32[512,256]{1,0:T(8,128)S(1)}, u32[]{:S(2)}) copy-start(f32[512,256]{1,0:T(8,128)S(1)} %bitcast_add_fusion) | copy-start | bytes 1572868
  126.6 55.4 %collective-permute-start.17 = (f32[2,3,256,128]{3,2,1,0:T(8,128)}, f32[2,3,256,128]{3,2,1,0:T(8,128)}, u32[]{:S(2)}, u32[]{:S(2)}) collective-permute-start(f32[2,3,256,128]{3,2,1,0:T(8,128)} %copy-done.11), channel_id=1, source_target_pairs={{0,4},{4,8},{8,12},{12,16},{16,20},{20,24},{24,28},{28,32},{32,36}... | collective-permute-start | bytes 2359304 | tf_op jit(solution)/shard_map/grad_4/ppermute | solution.py:344
  136.9 22.1 %collective-permute-start.10 = (f32[128,256]{1,0:T(8,128)}, f32[128,256]{1,0:T(8,128)}, u32[]{:S(2)}, u32[]{:S(2)}) collective-permute-start(f32[128,256]{1,0:T(8,128)} %get-tuple-element.88), channel_id=1, source_target_pairs={{0,2},{1,3},{2,0},{3,1},{4,6},{5,7},{6,4},{7,5},{8,10},{9,11},{10,... | collective-permute-start | bytes 393224 | tf_op jit(solution)/shard_map/swap_y1/ppermute | solution.py:373
  136.9 28.4 %collective-permute-start.11 = (f32[128,256]{1,0:T(8,128)}, f32[128,256]{1,0:T(8,128)}, u32[]{:S(2)}, u32[]{:S(2)}) collective-permute-start(f32[128,256]{1,0:T(8,128)} %get-tuple-element.87), channel_id=1, source_target_pairs={{0,64},{1,65},{2,66},{3,67},{4,68},{5,69},{6,70},{7,71},{8,72},{9,... | collective-permute-start | bytes 393224 | tf_op jit(solution)/shard_map/swap_y2/ppermute | solution.py:373
  158.6 8.9 %collective-permute-start.12 = (f32[128,256]{1,0:T(8,128)S(1)}, f32[128,256]{1,0:T(8,128)}, u32[]{:S(2)}, u32[]{:S(2)}) collective-permute-start(f32[128,256]{1,0:T(8,128)S(1)} %get-tuple-element.86), channel_id=1, source_target_pairs={{0,66},{1,67},{2,64},{3,65},{4,70},{5,71},{6,68},{7,69},{8,74},{9,... | collective-permute-start | bytes 393224 | tf_op jit(solution)/shard_map/swap_y3/ppermute | solution.py:373
  168.7 12.1 %collective-permute-start.15 = (f32[128,256]{1,0:T(8,128)S(1)}, f32[128,256]{1,0:T(8,128)S(1)}, u32[]{:S(2)}, u32[]{:S(2)}) collective-permute-start(f32[128,256]{1,0:T(8,128)S(1)} %fusion), channel_id=1, source_target_pairs={{0,32},{1,33},{2,34},{3,35},{4,36},{5,37},{6,38},{7,39},{8,40},{9,... | collective-permute-start | bytes 393224 | tf_op jit(solution)/shard_map/swap_z2/ppermute | solution.py:373
  168.8 12.4 %collective-permute-start.16 = (f32[128,256]{1,0:T(8,128)S(1)}, f32[128,256]{1,0:T(8,128)S(1)}, u32[]{:S(2)}, u32[]{:S(2)}) collective-permute-start(f32[128,256]{1,0:T(8,128)S(1)} %fusion), channel_id=1, source_target_pairs={{0,48},{1,49},{2,50},{3,51},{4,52},{5,53},{6,54},{7,55},{8,56},{9,... | collective-permute-start | bytes 393224 | tf_op jit(solution)/shard_map/swap_z3/ppermute | solution.py:373
  175.5 6.4 %collective-permute-start.14 = (f32[128,256]{1,0:T(8,128)S(1)}, f32[128,256]{1,0:T(8,128)S(1)}, u32[]{:S(2)}, u32[]{:S(2)}) collective-permute-start(f32[128,256]{1,0:T(8,128)S(1)} %fusion), channel_id=1, source_target_pairs={{0,16},{1,17},{2,18},{3,19},{4,20},{5,21},{6,22},{7,23},{8,24},{9,... | collective-permute-start | bytes 393224 | tf_op jit(solution)/shard_map/swap_z1/ppermute | solution.py:373
  176.0 23.9 %collective-permute-start.22 = (f32[2,2,256,128]{3,2,1,0:T(8,128)}, f32[2,2,256,128]{3,2,1,0:T(8,128)S(1)}, u32[]{:S(2)}, u32[]{:S(2)}) collective-permute-start(f32[2,2,256,128]{3,2,1,0:T(8,128)} %copy-done.12), channel_id=1, source_target_pairs={{0,5},{1,6},{2,7},{4,9},{5,10},{6,11},{8,13},{9,14},{10,15},{12,17... | collective-permute-start | bytes 1572872 | tf_op jit(solution)/shard_map/slant/ppermute | solution.py:353
  182.0 14.5 %collective-permute-start.20 = (f32[128,256]{1,0:T(8,128)S(1)}, f32[128,256]{1,0:T(8,128)S(1)}, u32[]{:S(2)}, u32[]{:S(2)}) collective-permute-start(f32[128,256]{1,0:T(8,128)S(1)} %add_add_fusion), channel_id=1, source_target_pairs={{0,8},{1,9},{2,10},{3,11},{4,12},{5,13},{6,14},{7,15},{8,0},{9,1},... | collective-permute-start | bytes 393224 | tf_op jit(solution)/shard_map/swap_x2/ppermute | solution.py:373
  184.9 14.9 %collective-permute-start.21 = (f32[128,256]{1,0:T(8,128)S(1)}, f32[128,256]{1,0:T(8,128)S(1)}, u32[]{:S(2)}, u32[]{:S(2)}) collective-permute-start(f32[128,256]{1,0:T(8,128)S(1)} %add_add_fusion), channel_id=1, source_target_pairs={{0,12},{1,13},{2,14},{3,15},{4,8},{5,9},{6,10},{7,11},{8,4},{9,5},... | collective-permute-start | bytes 393224 | tf_op jit(solution)/shard_map/swap_x3/ppermute | solution.py:373
  186.5 13.3 %collective-permute-start.19 = (f32[128,256]{1,0:T(8,128)S(1)}, f32[128,256]{1,0:T(8,128)S(1)}, u32[]{:S(2)}, u32[]{:S(2)}) collective-permute-start(f32[128,256]{1,0:T(8,128)S(1)} %add_add_fusion), channel_id=1, source_target_pairs={{0,4},{1,5},{2,6},{3,7},{4,0},{5,1},{6,2},{7,3},{8,12},{9,13},{10,... | collective-permute-start | bytes 393224 | tf_op jit(solution)/shard_map/swap_x1/ppermute | solution.py:373
  200.7 20.9 %collective-permute-start.24 = (f32[128,256]{1,0:T(8,128)S(1)}, f32[128,256]{1,0:T(8,128)}, u32[]{:S(2)}, u32[]{:S(2)}) collective-permute-start(f32[128,256]{1,0:T(8,128)S(1)} %add_multiply_fusion), channel_id=1, source_target_pairs={{0,64},{1,65},{2,66},{3,67},{4,68},{5,69},{6,70},{7,71},{8,72},{9,... | collective-permute-start | bytes 393224 | tf_op jit(solution)/shard_map/swap_y2/ppermute | solution.py:373
  211.4 10.2 %collective-permute-start.25 = (f32[128,256]{1,0:T(8,128)S(1)}, f32[128,256]{1,0:T(8,128)}, u32[]{:S(2)}, u32[]{:S(2)}) collective-permute-start(f32[128,256]{1,0:T(8,128)S(1)} %add_multiply_fusion), channel_id=1, source_target_pairs={{0,66},{1,67},{2,64},{3,65},{4,70},{5,71},{6,68},{7,69},{8,74},{9,... | collective-permute-start | bytes 393224 | tf_op jit(solution)/shard_map/swap_y3/ppermute | solution.py:373
  211.4 10.2 %collective-permute-start.23 = (f32[128,256]{1,0:T(8,128)S(1)}, f32[128,256]{1,0:T(8,128)}, u32[]{:S(2)}, u32[]{:S(2)}) collective-permute-start(f32[128,256]{1,0:T(8,128)S(1)} %add_multiply_fusion), channel_id=1, source_target_pairs={{0,2},{1,3},{2,0},{3,1},{4,6},{5,7},{6,4},{7,5},{8,10},{9,11},{10,... | collective-permute-start | bytes 393224 | tf_op jit(solution)/shard_map/swap_y1/ppermute | solution.py:373
  211.4 1.2 copy-start.4
  217.0 10.9 %collective-permute-start.18 = (f32[2,2,256,128]{3,2,1,0:T(8,128)}, f32[2,2,256,128]{3,2,1,0:T(8,128)S(1)}, u32[]{:S(2)}, u32[]{:S(2)}) collective-permute-start(f32[2,2,256,128]{3,2,1,0:T(8,128)} %get-tuple-element.66), channel_id=1, source_target_pairs={{0,1},{1,2},{2,3},{4,5},{5,6},{6,7},{8,9},{9,10},{10,11},{12,13},{... | collective-permute-start | bytes 1572872 | tf_op jit(solution)/shard_map/over/ppermute | solution.py:344
  222.7 8.6 %collective-permute-start.26 = (f32[512,256]{1,0:T(8,128)S(1)}, f32[512,256]{1,0:T(8,128)}, u32[]{:S(2)}, u32[]{:S(2)}) collective-permute-start(f32[512,256]{1,0:T(8,128)S(1)} %pad_maximum_fusion.2), channel_id=1, source_target_pairs={{0,1},{1,0},{2,3},{3,2},{4,5},{5,4},{6,7},{7,6},{8,9},{9,8},{10,11... | collective-permute-start | bytes 1572872 | tf_op jit(solution)/shard_map/swap_c1/ppermute | solution.py:373
  (18 other events, 17.1 us)

commit v3 on v0

--- a/solution.py
+++ b/solution.py
@@ -407,7 +407,7 @@
     return jnp.concatenate([part_of(i) for i in range(pieces)], 0)
 
 
-BOUNDS = (5, 9, 13, 15, 16)
+BOUNDS = (4, 8, 12, 15, 16)
 
 
 def shards(field, probe, measured, offsets, live):

time: 228 us -> 222 us (0.974)
  the two profiles are of different devices: /device:TPU:72 before, /device:TPU:1 now
where the time goes in v3:
time: 222 us; the launch traced here: 221 us
  starting transfers between devices  97.7 us (44%)
  Pallas kernels  42 us (19%)
  waiting for transfers between devices  41.2 us (19%)
  local copies, waits for them, and re-layouts  30.8 us (14%)
  other arithmetic  7.34 us (3%)
    ppermute x14, starting transfers between devices, swapped(): return lax.ppermute(array, AXES, pairs)  63 us
    pallas_call x5, Pallas kernels, run_group(): pl.pallas_call(functools.partial(group_kernel, first, count, (homes[0], h...  36.6 us
    ppermute x12, starting transfers between devices, shifted(): return lax.ppermute(array, axis, pairs)  33.4 us
    ppermute x12, waiting for transfers between devices, shifted(): return lax.ppermute(array, axis, pairs)  27.1 us
    unnamed x77, local copies, waits for them, and re-layouts  19.7 us
    ppermute x14, waiting for transfers between devices, swapped(): return lax.ppermute(array, AXES, pairs)  14 us
    pallas_call x2, Pallas kernels, finish(): pl.pallas_call(functools.partial(finish_kernel, tuple(blocks), terms), ou...  5.48 us
    slice x3, local copies, waits for them, and re-layouts, shards(): part = rest[:, :, LANE * a:LANE * b]  4.77 us
  transfers between devices with their start and end apart: 27, of which 8 were waited for; matrix products, arithmetic and copies ran while one was open for 6% of the time, Pallas kernels for 19%

profile of v3, /device:TPU:1, one launch (start us, length us, event | category | flops | bytes accessed | tf_op | source)
XLA Modules:
  0.0 221.0 jit_solution(2937382637256847652)
XLA Ops:
  0.6 2.4 %slice.21 = f32[2,256,512]{2,1,0:T(8,128)} slice(f32[2,256,2048]{2,1,0:T(8,128)} %refs_0_.9), slice={[0:2], [0:256], [0:512]} | slice | bytes 2097152 | tf_op jit(solution)/shard_map/slice | solution.py:420
  3.0 1.3 collective-permute-start
  4.3 3.1 %fusion.1 = (f32[2,256,512]{2,1,0:T(8,128)}, f32[2,256,512]{2,1,0:T(8,128)}) fusion(f32[2,256,2048]{2,1,0:T(8,128)} %refs_0_.9), kind=kLoop, calls=%fused_computation.20 | loop fusion | bytes 4194304 | tf_op jit(solution)/shard_map/slice | solution.py:423
  7.3 1.3 collective-permute-start.6
  9.6 1.6 reshape.17
  11.1 1.3 copy.13
  12.5 17.1 %collective-permute-done.refs_1_ = f32[2,256,512]{2,1,0:T(8,128)S(1)} collective-permute-done((f32[2,256,512]{2,1,0:T(8,128)}, f32[2,256,512]{2,1,0:T(8,128)S(1)}, u32[]{:S(2)}, u32[]{:S(2)}) %collective-permute-start) | collective-permute-done | bytes 1048608 | tf_op jit(solution)/shard_map/halo_0/ppermute | solution.py:344
  31.7 5.0 %group_0.1 = (f32[2,2,256,128]{3,2,1,0:T(8,128)S(1)}, f32[2,2,256,128]{3,2,1,0:T(8,128)}, f32[2,2,512,128]{3,2,1,0:T(8,128)S(1)}, f32[2,2,256,256]{3,2,1,0:T(8,128)S(1)}) custom-call(s32[1]{0:T(128)S(6)} %copy.15.live, s32[16,2]{1,0:T(8,128)S(1)} %broadcast_subtract_fusion.off, f32[2,256,2048]{2,1,0:T(8,128)} %refs_0_.9, ...), custom_call_target="tpu_custom_call" | custom-call | flops 8589934592 | bytes 4096 | tf_op jit(solution)/shard_map/group_0/pallas_call | solution.py:271
  36.7 5.5 %collective-permute-start.1 = (f32[2,2,256,128]{3,2,1,0:T(8,128)}, f32[2,2,256,128]{3,2,1,0:T(8,128)S(1)}, u32[]{:S(2)}, u32[]{:S(2)}) collective-permute-start(f32[2,2,256,128]{3,2,1,0:T(8,128)} %get-tuple-element.43), channel_id=1, source_target_pairs={{0,4},{4,8},{8,12},{12,16},{16,20},{20,24},{24,28},{28,32},{32,36}... | collective-permute-start | bytes 1572872 | tf_op jit(solution)/shard_map/grad_0/ppermute | solution.py:344
  42.2 1.3 collective-permute-start.5
  44.6 4.7 %collective-permute-start.4 = (f32[2,512,256]{2,1,0:T(8,128)}, f32[2,512,256]{2,1,0:T(8,128)}, u32[]{:S(2)}, u32[]{:S(2)}) collective-permute-start(f32[2,512,256]{2,1,0:T(8,128)} %pad_maximum_fusion), channel_id=1, source_target_pairs={{1,0},{2,1},{3,2},{5,4},{6,5},{7,6},{9,8},{10,9},{11,10},{13,12},{... | collective-permute-start | bytes 3145736 | tf_op jit(solution)/shard_map/corner/ppermute | solution.py:344
  49.3 2.8 %collective-permute-done.6.refs_2_.refs_1_ = f32[2,256,512]{2,1,0:T(8,128)} collective-permute-done((f32[2,256,512]{2,1,0:T(8,128)}, f32[2,256,512]{2,1,0:T(8,128)}, u32[]{:S(2)}, u32[]{:S(2)}) %collective-permute-start.6) | collective-permute-done | bytes 1048608 | tf_op jit(solution)/shard_map/halo_1/ppermute | solution.py:344
  52.1 8.5 %group_2.1 = (f32[2,4,256,128]{3,2,1,0:T(8,128)S(1)}, f32[2,4,256,128]{3,2,1,0:T(8,128)}, f32[2,2,512,128]{3,2,1,0:T(8,128)S(1)}, f32[2,2,256,256]{3,2,1,0:T(8,128)S(1)}) custom-call(s32[1]{0:T(128)S(6)} %copy.15.live, s32[16,2]{1,0:T(8,128)S(1)} %broadcast_subtract_fusion.off, f32[2,256,2048]{2,1,0:T(8,128)} %refs_0_.9, ...), custom_call_target="tpu_custom_call" | custom-call | flops 8589934592 | bytes 4096 | tf_op jit(solution)/shard_map/group_2/pallas_call | solution.py:271
  62.6 1.1 copy-done.30
  63.7 1.3 collective-permute-start.7
  66.0 1.3 collective-permute-start.2
  68.0 1.3 collective-permute-start.3
  69.3 5.2 %collective-permute-done.5.refs_2_.refs_1_ = f32[2,256,512]{2,1,0:T(8,128)} collective-permute-done((f32[2,256,512]{2,1,0:T(8,128)}, f32[2,256,512]{2,1,0:T(8,128)}, u32[]{:S(2)}, u32[]{:S(2)}) %collective-permute-start.5) | collective-permute-done | bytes 1048608 | tf_op jit(solution)/shard_map/halo_2/ppermute | solution.py:344
  77.6 8.8 %group_6.1 = (f32[2,4,256,128]{3,2,1,0:T(8,128)S(1)}, f32[2,4,256,128]{3,2,1,0:T(8,128)}, f32[2,2,512,128]{3,2,1,0:T(8,128)S(1)}, f32[2,2,256,256]{3,2,1,0:T(8,128)S(1)}) custom-call(s32[1]{0:T(128)S(6)} %copy.15.live, s32[16,2]{1,0:T(8,128)S(1)} %broadcast_subtract_fusion.off, f32[2,256,2048]{2,1,0:T(8,128)} %refs_0_.9, ...), custom_call_target="tpu_custom_call" | custom-call | flops 8589934592 | bytes 4096 | tf_op jit(solution)/shard_map/group_6/pallas_call | solution.py:271
  87.4 1.1 copy-done.27
  88.5 4.8 %collective-permute-start.9 = (f32[2,4,256,128]{3,2,1,0:T(8,128)}, f32[2,4,256,128]{3,2,1,0:T(8,128)}, u32[]{:S(2)}, u32[]{:S(2)}) collective-permute-start(f32[2,4,256,128]{3,2,1,0:T(8,128)} %get-tuple-element.56), channel_id=1, source_target_pairs={{0,4},{4,8},{8,12},{12,16},{16,20},{20,24},{24,28},{28,32},{32,36}... | collective-permute-start | bytes 3145736 | tf_op jit(solution)/shard_map/grad_2/ppermute | solution.py:344
  93.3 6.8 %group_10.1 = (f32[2,3,256,128]{3,2,1,0:T(8,128)S(1)}, f32[2,3,256,128]{3,2,1,0:T(8,128)}, f32[2,2,512,128]{3,2,1,0:T(8,128)S(1)}, f32[2,2,256,256]{3,2,1,0:T(8,128)S(1)}) custom-call(s32[1]{0:T(128)S(6)} %copy.15.live, s32[16,2]{1,0:T(8,128)S(1)} %broadcast_subtract_fusion.off, f32[2,256,2048]{2,1,0:T(8,128)} %refs_0_.9, ...), custom_call_target="tpu_custom_call" | custom-call | flops 8589934592 | bytes 4096 | tf_op jit(solution)/shard_map/group_10/pallas_call | solution.py:271
  102.1 7.4 %group_13.1 = (f32[2,3,256,128]{3,2,1,0:T(8,128)S(1)}, f32[2,3,256,128]{3,2,1,0:T(8,128)S(1)}, f32[2,2,256,128]{3,2,1,0:T(8,128)S(1)}, f32[2,2,256,128]{3,2,1,0:T(8,128)S(1)}, f32[2,2,256,256]{3,2,1,0:T(8,128)S(1)}) custom-call(s32[1]{0:T(128)S(6)} %copy.15.live, s32[16,2]{1,0:T(8,128)S(1)} %broadcast_subtract_fusion.off, f32[2,256,2048]{2,1,0:T(8,128)} %refs_0_.9, ...), custom_call_target="tpu_custom_call" | custom-call | flops 8589934592 | bytes 4096 | tf_op jit(solution)/shard_map/group_13/pallas_call | solution.py:271
  113.8 2.2 collective-permute-start.8
  116.0 2.2 collective-permute-start.13
  118.2 1.1 bitcast_add_fusion
  119.3 3.9 %collective-permute-start.17 = (f32[2,3,256,128]{3,2,1,0:T(8,128)}, f32[2,3,256,128]{3,2,1,0:T(8,128)}, u32[]{:S(2)}, u32[]{:S(2)}) collective-permute-start(f32[2,3,256,128]{3,2,1,0:T(8,128)} %copy-done.10), channel_id=1, source_target_pairs={{0,4},{4,8},{8,12},{12,16},{16,20},{20,24},{24,28},{28,32},{32,36}... | collective-permute-start | bytes 2359304 | tf_op jit(solution)/shard_map/grad_4/ppermute | solution.py:344
  123.2 15.7 %collective-permute-start.10 = (f32[128,256]{1,0:T(8,128)S(1)}, f32[128,256]{1,0:T(8,128)S(1)}, u32[]{:S(2)}, u32[]{:S(2)}) collective-permute-start(f32[128,256]{1,0:T(8,128)S(1)} %get-tuple-element.86), channel_id=1, source_target_pairs={{0,2},{1,3},{2,0},{3,1},{4,6},{5,7},{6,4},{7,5},{8,10},{9,11},{10,... | collective-permute-start | bytes 393224 | tf_op jit(solution)/shard_map/swap_y1/ppermute | solution.py:373
  138.9 3.9 %collective-permute-start.11 = (f32[128,256]{1,0:T(8,128)S(1)}, f32[128,256]{1,0:T(8,128)S(1)}, u32[]{:S(2)}, u32[]{:S(2)}) collective-permute-start(f32[128,256]{1,0:T(8,128)S(1)} %get-tuple-element.85), channel_id=1, source_target_pairs={{0,64},{1,65},{2,66},{3,67},{4,68},{5,69},{6,70},{7,71},{8,72},{9,... | collective-permute-start | bytes 393224 | tf_op jit(solution)/shard_map/swap_y2/ppermute | solution.py:373
  143.0 3.7 %collective-permute-done.11 = f32[128,256]{1,0:T(8,128)S(1)} collective-permute-done((f32[128,256]{1,0:T(8,128)S(1)}, f32[128,256]{1,0:T(8,128)S(1)}, u32[]{:S(2)}, u32[]{:S(2)}) %collective-permute-start.11) | collective-permute-done | bytes 131104 | tf_op jit(solution)/shard_map/swap_y2/ppermute | solution.py:373
  146.7 1.6 collective-permute-done.12
  149.2 4.4 %collective-permute-start.15 = (f32[128,256]{1,0:T(8,128)S(1)}, f32[128,256]{1,0:T(8,128)S(1)}, u32[]{:S(2)}, u32[]{:S(2)}) collective-permute-start(f32[128,256]{1,0:T(8,128)S(1)} %fusion), channel_id=1, source_target_pairs={{0,32},{1,33},{2,34},{3,35},{4,36},{5,37},{6,38},{7,39},{8,40},{9,... | collective-permute-start | bytes 393224 | tf_op jit(solution)/shard_map/swap_z2/ppermute | solution.py:373
  153.6 21.1 %collective-permute-start.16 = (f32[128,256]{1,0:T(8,128)S(1)}, f32[128,256]{1,0:T(8,128)S(1)}, u32[]{:S(2)}, u32[]{:S(2)}) collective-permute-start(f32[128,256]{1,0:T(8,128)S(1)} %fusion), channel_id=1, source_target_pairs={{0,48},{1,49},{2,50},{3,51},{4,52},{5,53},{6,54},{7,55},{8,56},{9,... | collective-permute-start | bytes 393224 | tf_op jit(solution)/shard_map/swap_z3/ppermute | solution.py:373
  175.2 1.3 collective-permute-start.22
  176.6 1.2 copy-done.3
  177.8 1.2 copy-done.5
  179.0 1.1 copy-done.9
  180.2 3.2 %finish_2.1.refs_6_ = f32[2,256,2048]{2,1,0:T(8,128)} custom-call(f32[2,2,256,128]{3,2,1,0:T(8,128)S(1)} %get-tuple-element.42.refs_0_, f32[2,2,256,128]{3,2,1,0:T(8,128)S(1)} %collective-permute-done.1.refs_3_.refs_1_, f32[2,4,256,128]{3,2,1,0:T(8,128)S(1)} %copy-done.1, f32[2,4,256,128]{3,2,1,0:T(8,128)S(1)} %copy-done.3, ...), custom_call_target="tpu_custom_call" | custom-call | tf_op jit(solution)/shard_map/finish_2/pallas_call | solution.py:325
  183.6 7.3 %collective-permute-start.21 = (f32[128,256]{1,0:T(8,128)S(1)}, f32[128,256]{1,0:T(8,128)S(1)}, u32[]{:S(2)}, u32[]{:S(2)}) collective-permute-start(f32[128,256]{1,0:T(8,128)S(1)} %add_add_fusion), channel_id=1, source_target_pairs={{0,12},{1,13},{2,14},{3,15},{4,8},{5,9},{6,10},{7,11},{8,4},{9,5},... | collective-permute-start | bytes 393224 | tf_op jit(solution)/shard_map/swap_x3/ppermute | solution.py:373
  191.4 7.7 %collective-permute-done.21 = f32[128,256]{1,0:T(8,128)S(1)} collective-permute-done((f32[128,256]{1,0:T(8,128)S(1)}, f32[128,256]{1,0:T(8,128)S(1)}, u32[]{:S(2)}, u32[]{:S(2)}) %collective-permute-start.21) | collective-permute-done | bytes 131104 | tf_op jit(solution)/shard_map/swap_x3/ppermute | solution.py:373
  199.1 5.5 %collective-permute-start.24 = (f32[128,256]{1,0:T(8,128)S(1)}, f32[128,256]{1,0:T(8,128)S(1)}, u32[]{:S(2)}, u32[]{:S(2)}) collective-permute-start(f32[128,256]{1,0:T(8,128)S(1)} %add_multiply_fusion), channel_id=1, source_target_pairs={{0,64},{1,65},{2,66},{3,67},{4,68},{5,69},{6,70},{7,71},{8,72},{9,... | collective-permute-start | bytes 393224 | tf_op jit(solution)/shard_map/swap_y2/ppermute | solution.py:373
  204.6 4.5 %collective-permute-start.18 = (f32[2,2,256,128]{3,2,1,0:T(8,128)}, f32[2,2,256,128]{3,2,1,0:T(8,128)S(1)}, u32[]{:S(2)}, u32[]{:S(2)}) collective-permute-start(f32[2,2,256,128]{3,2,1,0:T(8,128)} %copy-done.11), channel_id=1, source_target_pairs={{0,1},{1,2},{2,3},{4,5},{5,6},{6,7},{8,9},{9,10},{10,11},{12,13},{... | collective-permute-start | bytes 1572872 | tf_op jit(solution)/shard_map/over/ppermute | solution.py:344
  209.2 1.0 collective-permute-done.25
  210.8 1.1 select_select_fusion.3
  212.8 1.7 collective-permute-start.26
  214.5 2.0 collective-permute-done.18.refs_4_
  216.5 2.3 %finish_0.1 = f32[2,256,2048]{2,1,0:T(8,128)} custom-call(f32[2,2,256,128]{3,2,1,0:T(8,128)S(1)} %get-tuple-element.42.refs_0_, f32[2,2,256,128]{3,2,1,0:T(8,128)S(1)} %collective-permute-done.1.refs_3_.refs_1_, f32[2,3,256,128]{3,2,1,0:T(8,128)S(1)} %copy-done.7, ...), custom_call_target="tpu_custom_call", output_to_operand_aliasing={{}: (6, {})} | custom-call | tf_op jit(solution)/shard_map/finish_0/pallas_call | solution.py:325
  218.8 1.1 broadcast_select_fusion.1
  (114 shorter events, 22.1 us)
Async XLA Ops:
  0.6 8.0 %copy-start.37 = (s32[16,2]{0,1:T(2,128)S(1)}, s32[16,2]{0,1:T(2,128)}, u32[]{:S(2)}) copy-start(s32[16,2]{0,1:T(2,128)} %param.12) | copy-start | bytes 388
  0.6 8.9 %copy-start.34 = (f32[2,2,256,256]{3,2,1,0:T(8,128)S(1)}, f32[2,2,256,256]{3,2,1,0:T(8,128)}, u32[]{:S(2)}) copy-start(f32[2,2,256,256]{3,2,1,0:T(8,128)} %param.10) | copy-start | bytes 3145732
  3.0 26.5 %collective-permute-start = (f32[2,256,512]{2,1,0:T(8,128)}, f32[2,256,512]{2,1,0:T(8,128)S(1)}, u32[]{:S(2)}, u32[]{:S(2)}) collective-permute-start(f32[2,256,512]{2,1,0:T(8,128)} %slice.21), channel_id=1, source_target_pairs={{4,0},{8,4},{12,8},{16,12},{20,16},{24,20},{28,24},{32,28},{36,32}... | collective-permute-start | bytes 3145736 | tf_op jit(solution)/shard_map/halo_0/ppermute | solution.py:344
  7.3 44.7 %collective-permute-start.6 = (f32[2,256,512]{2,1,0:T(8,128)}, f32[2,256,512]{2,1,0:T(8,128)}, u32[]{:S(2)}, u32[]{:S(2)}) collective-permute-start(f32[2,256,512]{2,1,0:T(8,128)} %get-tuple-element.76), channel_id=1, source_target_pairs={{4,0},{8,4},{12,8},{16,12},{20,16},{24,20},{28,24},{32,28},{36,32}... | collective-permute-start | bytes 3145736 | tf_op jit(solution)/shard_map/halo_1/ppermute | solution.py:344
  8.8 20.9 %copy-start.13 = (bf16[512,512]{1,0:T(8,128)(2,1)S(1)}, bf16[512,512]{1,0:T(8,128)(2,1)}, u32[]{:S(2)}) copy-start(bf16[512,512]{1,0:T(8,128)(2,1)} %constant.82.clone.refs_5_.refs_6_.refs_7_.refs_8_) | copy-start | bytes 1572868
  8.8 20.9 %copy-start.21 = (bf16[2,256,256]{2,1,0:T(8,128)(2,1)S(1)}, bf16[2,256,256]{2,1,0:T(8,128)(2,1)}, u32[]{:S(2)}) copy-start(bf16[2,256,256]{2,1,0:T(8,128)(2,1)} %constant.81.clone.refs_4_.refs_5_.refs_6_.refs_7_) | copy-start | bytes 786436
  31.7 11.8 %slice-start = ((f32[2,256,2048]{2,1,0:T(8,128)}), f32[2,256,256]{2,1,0:T(8,128)S(1)}, s32[]{:S(2)}) async-start(f32[2,256,2048]{2,1,0:T(8,128)} %refs_0_.9), calls=%async_computation | async-start | bytes 1048576 | tf_op jit(solution)/shard_map/slice | solution.py:427
  31.7 20.4 %copy-start.14 = (bf16[512,512]{1,0:T(8,128)(2,1)S(1)}, bf16[512,512]{1,0:T(8,128)(2,1)}, u32[]{:S(2)}) copy-start(bf16[512,512]{1,0:T(8,128)(2,1)} %constant.82.clone.refs_5_.refs_6_.refs_7_.refs_8_) | copy-start | bytes 1572868
  31.7 20.4 %copy-start.18 = (bf16[512,512]{1,0:T(8,128)(2,1)S(1)}, bf16[512,512]{1,0:T(8,128)(2,1)}, u32[]{:S(2)}) copy-start(bf16[512,512]{1,0:T(8,128)(2,1)} %constant.84.clone.refs_7_.refs_8_.refs_9_.refs_10_) | copy-start | bytes 1572868
  31.7 20.4 %copy-start.23 = (bf16[2,256,256]{2,1,0:T(8,128)(2,1)S(1)}, bf16[2,256,256]{2,1,0:T(8,128)(2,1)}, u32[]{:S(2)}) copy-start(bf16[2,256,256]{2,1,0:T(8,128)(2,1)} %constant.83.clone.refs_6_.refs_7_.refs_8_.refs_9_) | copy-start | bytes 786436
  36.7 15.4 %copy-start.31 = (f32[2,2,256,256]{3,2,1,0:T(8,128)}, f32[2,2,256,256]{3,2,1,0:T(8,128)S(1)}, u32[]{:S(2)}) copy-start(f32[2,2,256,256]{3,2,1,0:T(8,128)S(1)} %get-tuple-element.46.refs_10_) | copy-start | bytes 3145732
  36.7 31.3 %collective-permute-start.1 = (f32[2,2,256,128]{3,2,1,0:T(8,128)}, f32[2,2,256,128]{3,2,1,0:T(8,128)S(1)}, u32[]{:S(2)}, u32[]{:S(2)}) collective-permute-start(f32[2,2,256,128]{3,2,1,0:T(8,128)} %get-tuple-element.43), channel_id=1, source_target_pairs={{0,4},{4,8},{8,12},{12,16},{16,20},{20,24},{24,28},{28,32},{32,36}... | collective-permute-start | bytes 1572872 | tf_op jit(solution)/shard_map/grad_0/ppermute | solution.py:344
  42.2 32.3 %collective-permute-start.5 = (f32[2,256,512]{2,1,0:T(8,128)}, f32[2,256,512]{2,1,0:T(8,128)}, u32[]{:S(2)}, u32[]{:S(2)}) collective-permute-start(f32[2,256,512]{2,1,0:T(8,128)} %get-tuple-element.44), channel_id=1, source_target_pairs={{4,0},{8,4},{12,8},{16,12},{20,16},{24,20},{28,24},{32,28},{36,32}... | collective-permute-start | bytes 3145736 | tf_op jit(solution)/shard_map/halo_2/ppermute | solution.py:344
  44.6 48.7 %collective-permute-start.4 = (f32[2,512,256]{2,1,0:T(8,128)}, f32[2,512,256]{2,1,0:T(8,128)}, u32[]{:S(2)}, u32[]{:S(2)}) collective-permute-start(f32[2,512,256]{2,1,0:T(8,128)} %pad_maximum_fusion), channel_id=1, source_target_pairs={{1,0},{2,1},{3,2},{5,4},{6,5},{7,6},{9,8},{10,9},{11,10},{13,12},{... | collective-permute-start | bytes 3145736 | tf_op jit(solution)/shard_map/corner/ppermute | solution.py:344
  52.1 12.9 %copy-start.32 = (f32[2,256,2048]{2,1,0:T(8,128)S(1)}, f32[2,256,2048]{2,1,0:T(8,128)}, u32[]{:S(2)}) copy-start(f32[2,256,2048]{2,1,0:T(8,128)} %refs_0_.9) | copy-start | bytes 12582916
  63.7 29.6 %collective-permute-start.7 = (f32[2,4,256,128]{3,2,1,0:T(8,128)}, f32[2,4,256,128]{3,2,1,0:T(8,128)S(1)}, u32[]{:S(2)}, u32[]{:S(2)}) collective-permute-start(f32[2,4,256,128]{3,2,1,0:T(8,128)} %get-tuple-element.47), channel_id=1, source_target_pairs={{0,4},{4,8},{8,12},{12,16},{16,20},{20,24},{24,28},{28,32},{32,36}... | collective-permute-start | bytes 3145736 | tf_op jit(solution)/shard_map/grad_1/ppermute | solution.py:344
  66.0 27.3 %collective-permute-start.2 = (f32[2,256,384]{2,1,0:T(8,128)}, f32[2,256,384]{2,1,0:T(8,128)}, u32[]{:S(2)}, u32[]{:S(2)}) collective-permute-start(f32[2,256,384]{2,1,0:T(8,128)} %slice.23), channel_id=1, source_target_pairs={{4,0},{8,4},{12,8},{16,12},{20,16},{24,20},{28,24},{32,28},{36,32}... | collective-permute-start | bytes 2359304 | tf_op jit(solution)/shard_map/halo_3/ppermute | solution.py:344
  68.0 34.0 %collective-permute-start.3 = (f32[2,256,128]{2,1,0:T(8,128)}, f32[2,256,128]{2,1,0:T(8,128)S(1)}, u32[]{:S(2)}, u32[]{:S(2)}) collective-permute-start(f32[2,256,128]{2,1,0:T(8,128)} %slice.24), channel_id=1, source_target_pairs={{4,0},{8,4},{12,8},{16,12},{20,16},{24,20},{28,24},{32,28},{36,32}... | collective-permute-start | bytes 786440 | tf_op jit(solution)/shard_map/halo_4/ppermute | solution.py:344
  77.6 15.7 %copy-start.16 = (bf16[512,512]{1,0:T(8,128)(2,1)S(1)}, bf16[512,512]{1,0:T(8,128)(2,1)}, u32[]{:S(2)}) copy-start(bf16[512,512]{1,0:T(8,128)(2,1)} %constant.82.clone.refs_5_.refs_6_.refs_7_.refs_8_) | copy-start | bytes 1572868
  77.6 15.7 %copy-start.20 = (bf16[512,512]{1,0:T(8,128)(2,1)S(1)}, bf16[512,512]{1,0:T(8,128)(2,1)}, u32[]{:S(2)}) copy-start(bf16[512,512]{1,0:T(8,128)(2,1)} %constant.84.clone.refs_7_.refs_8_.refs_9_.refs_10_) | copy-start | bytes 1572868
  77.6 15.7 %copy-start.25 = (bf16[2,256,256]{2,1,0:T(8,128)(2,1)S(1)}, bf16[2,256,256]{2,1,0:T(8,128)(2,1)}, u32[]{:S(2)}) copy-start(bf16[2,256,256]{2,1,0:T(8,128)(2,1)} %constant.83.clone.refs_6_.refs_7_.refs_8_.refs_9_) | copy-start | bytes 786436
  88.5 11.7 %copy-start.4 = (f32[2,4,256,128]{3,2,1,0:T(8,128)}, f32[2,4,256,128]{3,2,1,0:T(8,128)S(1)}, u32[]{:S(2)}) copy-start(f32[2,4,256,128]{3,2,1,0:T(8,128)S(1)} %get-tuple-element.64.refs_4_) | copy-start | bytes 3145732
  88.5 30.8 %collective-permute-start.9 = (f32[2,4,256,128]{3,2,1,0:T(8,128)}, f32[2,4,256,128]{3,2,1,0:T(8,128)}, u32[]{:S(2)}, u32[]{:S(2)}) collective-permute-start(f32[2,4,256,128]{3,2,1,0:T(8,128)} %get-tuple-element.56), channel_id=1, source_target_pairs={{0,4},{4,8},{8,12},{12,16},{16,20},{20,24},{24,28},{28,32},{32,36}... | collective-permute-start | bytes 3145736 | tf_op jit(solution)/shard_map/grad_2/ppermute | solution.py:344
  93.3 6.9 %copy-start.2 = (f32[2,4,256,128]{3,2,1,0:T(8,128)}, f32[2,4,256,128]{3,2,1,0:T(8,128)S(1)}, u32[]{:S(2)}) copy-start(f32[2,4,256,128]{3,2,1,0:T(8,128)S(1)} %collective-permute-done.7.refs_3_) | copy-start | bytes 3145732
  112.9 63.6 %copy-start.1 = (f32[2,4,256,128]{3,2,1,0:T(8,128)S(1)}, f32[2,4,256,128]{3,2,1,0:T(8,128)}, u32[]{:S(2)}) copy-start(f32[2,4,256,128]{3,2,1,0:T(8,128)} %copy-done) | copy-start | bytes 3145732
  113.8 4.4 %collective-permute-start.8 = (f32[512,256]{1,0:T(8,128)}, f32[512,256]{1,0:T(8,128)}, u32[]{:S(2)}, u32[]{:S(2)}) collective-permute-start(f32[512,256]{1,0:T(8,128)} %dynamic-slice_bitcast_fusion), channel_id=1, source_target_pairs={{0,1},{1,0},{2,3},{3,2},{4,5},{5,4},{6,7},{7,6},{8,9},{9,8},{10,11... | collective-permute-start | bytes 1572872 | tf_op jit(solution)/shard_map/swap_c1/ppermute | solution.py:373
  116.0 33.2 %collective-permute-start.13 = (f32[2,3,256,128]{3,2,1,0:T(8,128)}, f32[2,3,256,128]{3,2,1,0:T(8,128)}, u32[]{:S(2)}, u32[]{:S(2)}) collective-permute-start(f32[2,3,256,128]{3,2,1,0:T(8,128)} %get-tuple-element.59), channel_id=1, source_target_pairs={{0,4},{4,8},{8,12},{12,16},{16,20},{20,24},{24,28},{28,32},{32,36}... | collective-permute-start | bytes 2359304 | tf_op jit(solution)/shard_map/grad_3/ppermute | solution.py:344
  119.3 3.9 %copy-start.33 = (f32[512,256]{1,0:T(8,128)}, f32[512,256]{1,0:T(8,128)S(1)}, u32[]{:S(2)}) copy-start(f32[512,256]{1,0:T(8,128)S(1)} %bitcast_add_fusion) | copy-start | bytes 1572868
  119.3 64.2 %collective-permute-start.17 = (f32[2,3,256,128]{3,2,1,0:T(8,128)}, f32[2,3,256,128]{3,2,1,0:T(8,128)}, u32[]{:S(2)}, u32[]{:S(2)}) collective-permute-start(f32[2,3,256,128]{3,2,1,0:T(8,128)} %copy-done.10), channel_id=1, source_target_pairs={{0,4},{4,8},{8,12},{12,16},{16,20},{20,24},{24,28},{28,32},{32,36}... | collective-permute-start | bytes 2359304 | tf_op jit(solution)/shard_map/grad_4/ppermute | solution.py:344
  123.2 19.7 %collective-permute-start.10 = (f32[128,256]{1,0:T(8,128)S(1)}, f32[128,256]{1,0:T(8,128)S(1)}, u32[]{:S(2)}, u32[]{:S(2)}) collective-permute-start(f32[128,256]{1,0:T(8,128)S(1)} %get-tuple-element.86), channel_id=1, source_target_pairs={{0,2},{1,3},{2,0},{3,1},{4,6},{5,7},{6,4},{7,5},{8,10},{9,11},{10,... | collective-permute-start | bytes 393224 | tf_op jit(solution)/shard_map/swap_y1/ppermute | solution.py:373
  138.9 7.8 %collective-permute-start.11 = (f32[128,256]{1,0:T(8,128)S(1)}, f32[128,256]{1,0:T(8,128)S(1)}, u32[]{:S(2)}, u32[]{:S(2)}) collective-permute-start(f32[128,256]{1,0:T(8,128)S(1)} %get-tuple-element.85), channel_id=1, source_target_pairs={{0,64},{1,65},{2,66},{3,67},{4,68},{5,69},{6,70},{7,71},{8,72},{9,... | collective-permute-start | bytes 393224 | tf_op jit(solution)/shard_map/swap_y2/ppermute | solution.py:373
  142.8 5.5 %collective-permute-start.12 = (f32[128,256]{1,0:T(8,128)S(1)}, f32[128,256]{1,0:T(8,128)S(1)}, u32[]{:S(2)}, u32[]{:S(2)}) collective-permute-start(f32[128,256]{1,0:T(8,128)S(1)} %get-tuple-element.84), channel_id=1, source_target_pairs={{0,66},{1,67},{2,64},{3,65},{4,70},{5,71},{6,68},{7,69},{8,74},{9,... | collective-permute-start | bytes 393224 | tf_op jit(solution)/shard_map/swap_y3/ppermute | solution.py:373
  149.2 34.2 %collective-permute-start.15 = (f32[128,256]{1,0:T(8,128)S(1)}, f32[128,256]{1,0:T(8,128)S(1)}, u32[]{:S(2)}, u32[]{:S(2)}) collective-permute-start(f32[128,256]{1,0:T(8,128)S(1)} %fusion), channel_id=1, source_target_pairs={{0,32},{1,33},{2,34},{3,35},{4,36},{5,37},{6,38},{7,39},{8,40},{9,... | collective-permute-start | bytes 393224 | tf_op jit(solution)/shard_map/swap_z2/ppermute | solution.py:373
  153.6 29.8 %collective-permute-start.16 = (f32[128,256]{1,0:T(8,128)S(1)}, f32[128,256]{1,0:T(8,128)S(1)}, u32[]{:S(2)}, u32[]{:S(2)}) collective-permute-start(f32[128,256]{1,0:T(8,128)S(1)} %fusion), channel_id=1, source_target_pairs={{0,48},{1,49},{2,50},{3,51},{4,52},{5,53},{6,54},{7,55},{8,56},{9,... | collective-permute-start | bytes 393224 | tf_op jit(solution)/shard_map/swap_z3/ppermute | solution.py:373
  174.8 8.6 %collective-permute-start.14 = (f32[128,256]{1,0:T(8,128)S(1)}, f32[128,256]{1,0:T(8,128)S(1)}, u32[]{:S(2)}, u32[]{:S(2)}) collective-permute-start(f32[128,256]{1,0:T(8,128)S(1)} %fusion), channel_id=1, source_target_pairs={{0,16},{1,17},{2,18},{3,19},{4,20},{5,21},{6,22},{7,23},{8,24},{9,... | collective-permute-start | bytes 393224 | tf_op jit(solution)/shard_map/swap_z1/ppermute | solution.py:373
  175.2 23.9 %collective-permute-start.22 = (f32[2,2,256,128]{3,2,1,0:T(8,128)}, f32[2,2,256,128]{3,2,1,0:T(8,128)S(1)}, u32[]{:S(2)}, u32[]{:S(2)}) collective-permute-start(f32[2,2,256,128]{3,2,1,0:T(8,128)} %copy-done.12), channel_id=1, source_target_pairs={{0,5},{1,6},{2,7},{4,9},{5,10},{6,11},{8,13},{9,14},{10,15},{12,17... | collective-permute-start | bytes 1572872 | tf_op jit(solution)/shard_map/slant/ppermute | solution.py:353
  176.6 1.2 copy-start.3
  177.8 1.2 copy-start.5
  179.0 1.1 copy-start.9
  180.2 36.4 %copy-start.7 = (f32[2,3,256,128]{3,2,1,0:T(8,128)S(1)}, f32[2,3,256,128]{3,2,1,0:T(8,128)}, u32[]{:S(2)}) copy-start(f32[2,3,256,128]{3,2,1,0:T(8,128)} %copy-done.6) | copy-start | bytes 2359300
  183.5 7.9 %collective-permute-start.20 = (f32[128,256]{1,0:T(8,128)S(1)}, f32[128,256]{1,0:T(8,128)S(1)}, u32[]{:S(2)}, u32[]{:S(2)}) collective-permute-start(f32[128,256]{1,0:T(8,128)S(1)} %add_add_fusion), channel_id=1, source_target_pairs={{0,8},{1,9},{2,10},{3,11},{4,12},{5,13},{6,14},{7,15},{8,0},{9,1},... | collective-permute-start | bytes 393224 | tf_op jit(solution)/shard_map/swap_x2/ppermute | solution.py:373
  183.6 15.5 %collective-permute-start.21 = (f32[128,256]{1,0:T(8,128)S(1)}, f32[128,256]{1,0:T(8,128)S(1)}, u32[]{:S(2)}, u32[]{:S(2)}) collective-permute-start(f32[128,256]{1,0:T(8,128)S(1)} %add_add_fusion), channel_id=1, source_target_pairs={{0,12},{1,13},{2,14},{3,15},{4,8},{5,9},{6,10},{7,11},{8,4},{9,5},... | collective-permute-start | bytes 393224 | tf_op jit(solution)/shard_map/swap_x3/ppermute | solution.py:373
  190.9 8.2 %collective-permute-start.19 = (f32[128,256]{1,0:T(8,128)S(1)}, f32[128,256]{1,0:T(8,128)S(1)}, u32[]{:S(2)}, u32[]{:S(2)}) collective-permute-start(f32[128,256]{1,0:T(8,128)S(1)} %add_add_fusion), channel_id=1, source_target_pairs={{0,4},{1,5},{2,6},{3,7},{4,0},{5,1},{6,2},{7,3},{8,12},{9,13},{10,... | collective-permute-start | bytes 393224 | tf_op jit(solution)/shard_map/swap_x1/ppermute | solution.py:373
  199.1 10.0 %collective-permute-start.24 = (f32[128,256]{1,0:T(8,128)S(1)}, f32[128,256]{1,0:T(8,128)S(1)}, u32[]{:S(2)}, u32[]{:S(2)}) collective-permute-start(f32[128,256]{1,0:T(8,128)S(1)} %add_multiply_fusion), channel_id=1, source_target_pairs={{0,64},{1,65},{2,66},{3,67},{4,68},{5,69},{6,70},{7,71},{8,72},{9,... | collective-permute-start | bytes 393224 | tf_op jit(solution)/shard_map/swap_y2/ppermute | solution.py:373
  204.6 5.6 %collective-permute-start.25 = (f32[128,256]{1,0:T(8,128)S(1)}, f32[128,256]{1,0:T(8,128)S(1)}, u32[]{:S(2)}, u32[]{:S(2)}) collective-permute-start(f32[128,256]{1,0:T(8,128)S(1)} %add_multiply_fusion), channel_id=1, source_target_pairs={{0,66},{1,67},{2,64},{3,65},{4,70},{5,71},{6,68},{7,69},{8,74},{9,... | collective-permute-start | bytes 393224 | tf_op jit(solution)/shard_map/swap_y3/ppermute | solution.py:373
  204.6 6.2 %collective-permute-start.23 = (f32[128,256]{1,0:T(8,128)S(1)}, f32[128,256]{1,0:T(8,128)}, u32[]{:S(2)}, u32[]{:S(2)}) collective-permute-start(f32[128,256]{1,0:T(8,128)S(1)} %add_multiply_fusion), channel_id=1, source_target_pairs={{0,2},{1,3},{2,0},{3,1},{4,6},{5,7},{6,4},{7,5},{8,10},{9,11},{10,... | collective-permute-start | bytes 393224 | tf_op jit(solution)/shard_map/swap_y1/ppermute | solution.py:373
  204.6 11.9 %collective-permute-start.18 = (f32[2,2,256,128]{3,2,1,0:T(8,128)}, f32[2,2,256,128]{3,2,1,0:T(8,128)S(1)}, u32[]{:S(2)}, u32[]{:S(2)}) collective-permute-start(f32[2,2,256,128]{3,2,1,0:T(8,128)} %copy-done.11), channel_id=1, source_target_pairs={{0,1},{1,2},{2,3},{4,5},{5,6},{6,7},{8,9},{9,10},{10,11},{12,13},{... | collective-permute-start | bytes 1572872 | tf_op jit(solution)/shard_map/over/ppermute | solution.py:344
  212.8 6.0 %collective-permute-start.26 = (f32[512,256]{1,0:T(8,128)}, f32[512,256]{1,0:T(8,128)}, u32[]{:S(2)}, u32[]{:S(2)}) collective-permute-start(f32[512,256]{1,0:T(8,128)} %pad_maximum_fusion.2), channel_id=1, source_target_pairs={{0,1},{1,0},{2,3},{3,2},{4,5},{5,4},{6,7},{7,6},{8,9},{9,8},{10,11... | collective-permute-start | bytes 1572872 | tf_op jit(solution)/shard_map/swap_c1/ppermute | solution.py:373
  (18 other events, 17.1 us)
